TPU v7x, 512 devices: a whole 4x8x8 slice. The times are simulated.
512 devices in a mesh: slab: 128 (over y, z, core), sub: 4 (over x).
Axes of the slice: x: 4, y: 8, z: 8, core: 2. Of those that a mesh axis runs over, the one named last changes fastest.
Arguments:
- leaves: bfloat16 [131072, 512], P(('slab', 'sub')), may hold values from -6 to 6
- m2l_ops: bfloat16 [16, 512, 512], P('sub'), may hold values from -0.09375 to 0.09375
- send_index: int32 [128, 128, 8], P('slab'), may hold values from 0 to 127
- pair_target: int32 [128, 16, 128], P('slab', 'sub'), may hold values from 0 to 127, each once within a row
- pair_source: int32 [128, 16, 128], P('slab', 'sub'), may hold values from 0 to 1151
- pair_count: int32 [128, 16], P('slab', 'sub'), may hold values from 25 to 128, as said below
Outputs:
- parent_multipoles: bfloat16 [16384, 512], P(('slab', 'sub'))
- local_expansions: float32 [16384, 512], P(('slab', 'sub'))
Inputs may be any that keep to these rules, and one draw needn't show every extreme that they name: `pair_count`: in every segment at least one operator, has all 128 slots live.
All inputs are finite; a program needn't handle non-finite values.
Results may differ from a plain program's by a relative error of at most 0.014.
Values may be sent and summed in bfloat16 or wider, within the bound.
No kernel may reach another device: no remote copies, remote signals or barrier semaphores. Data moves between devices by JAX's collectives and lax.ppermute only.
A program may use at most 64 MiB of HBM per device.

v0:
```python
import math

import jax
import jax.numpy as jnp
from jax import lax
from jax.sharding import PartitionSpec as P

ORDER = 8


def one_side(order, side):
    counter = jnp.arange(order, dtype=jnp.float32)
    angles = (2.0 * counter + 1.0) * math.pi / (2.0 * order)
    nodes = jnp.cos(angles)
    degree = jnp.arange(1, order, dtype=jnp.float32)
    parent_poly = jnp.cos(degree[:, None] * angles[None, :])
    child_pts = (nodes + (2.0 * side - 1.0)) / 2.0
    child_poly = jnp.cos(degree[:, None] * jnp.arccos(child_pts)[None, :])
    summed = jnp.sum(parent_poly[:, :, None] * child_poly[:, None, :], axis=0)
    return 1.0 / order + 2.0 / order * summed


def upward_matrix(order):
    sides = [one_side(order, 0), one_side(order, 1)]
    blocks = []
    for octant in range(8):
        first = sides[octant >> 2 & 1]
        second = sides[octant >> 1 & 1]
        third = sides[octant & 1]
        blocks.append(jnp.kron(first, jnp.kron(second, third)).T)
    return jnp.concatenate(blocks, axis=0).astype(jnp.bfloat16)


def body(leaves, m2l_ops, send_index, pair_target, pair_source, pair_count):
    width = leaves.shape[1]
    weights = upward_matrix(ORDER)
    parents = jnp.dot(
        leaves.reshape(leaves.shape[0] // 8, 8 * width), weights, preferred_element_type=jnp.float32
    ).astype(jnp.bfloat16)
    segment = lax.all_gather(parents, "sub", axis=0, tiled=True)
    seg_cells = segment.shape[0]
    picked = jnp.take(segment, send_index[0], axis=0)
    ghosts = lax.all_to_all(picked, "slab", split_axis=0, concat_axis=0, tiled=True)
    table = jnp.concatenate([segment, ghosts.reshape(-1, width)], axis=0)
    slot_ids = jnp.arange(pair_target.shape[2], dtype=jnp.int32)
    sources = jnp.take(table, pair_source[0], axis=0)
    images = jnp.einsum("kcn,kmn->kcm", sources, m2l_ops, preferred_element_type=jnp.float32)
    live = (slot_ids[None, :] < pair_count[0][:, None]).astype(jnp.float32)
    images = images * live[:, :, None]
    total = jnp.zeros((seg_cells, width), jnp.float32)
    total = total.at[pair_target[0].reshape(-1)].add(images.reshape(-1, width))
    local = lax.psum_scatter(
        total.astype(jnp.bfloat16), "sub", scatter_dimension=0, tiled=True
    ).astype(jnp.float32)
    return (parents, local)


def solution(mesh):
    in_specs = (
        P(("slab", "sub"), None),
        P("sub", None, None),
        P("slab", None, None),
        P("slab", "sub", None),
        P("slab", "sub", None),
        P("slab", "sub"),
    )
    out_specs = (P(("slab", "sub"), None), P(("slab", "sub"), None))
    return jax.shard_map(body, mesh=mesh, in_specs=in_specs, out_specs=out_specs, check_vma=False)
```

profile of v0, /device:TPU:1, one launch (start us, length us, event | category | flops | bytes accessed | tf_op | source)
XLA Modules:
  0.0 144.6 jit_solution(6535008525868307500)
XLA Ops:
  7.2 0.0 copy-start
  7.2 0.1 sqrt_atan2_fusion
  7.3 0.8 compare_and_fusion
  8.1 0.7 compare_select_fusion.1
  8.8 0.1 multiply_cosine_fusion.1
  8.9 0.1 multiply_reduce_fusion
  9.0 0.7 copy.11
  9.8 0.1 copy.12
  9.9 0.1 reshape.370
  10.0 1.1 reshape.365
  11.0 0.1 broadcast_multiply_fusion.1
  11.2 0.1 mul.395
  11.3 0.1 mul.389
  11.5 0.1 mul.400
  11.6 0.1 mul.378
  11.7 3.9 %multiply_convert_fusion.3 = (bf16[8,64,8,64]{3,2,1,0:T(8,128)(2,1)}, bf16[8,64,8,64]{3,2,1,0:T(8,128)(2,1)}, bf16[8,64,8,64]{3,2,1,0:T(8,128)(2,1)}, bf16[8,64,...) fusion(f32[8,8]{1,0:T(8,128)S(1)} %multiply_add_fusion, ...), kind=kLoop, calls=%fused_computation.6 | loop fusion | flops 4194304 | bytes 4260352 | tf_op jit(solution)/shard_map/convert.15
  15.7 2.6 %mul.406 = bf16[512,512]{1,0:T(8,128)(2,1)} reshape(bf16[8,64,8,64]{3,2,1,0:T(8,128)(2,1)} %get-tuple-element.10) | data formatting | bytes 1048576 | tf_op jit(solution)/shard_map/jit(kron)/mul | solution.py:30
  18.2 2.6 %mul.381 = bf16[512,512]{1,0:T(8,128)(2,1)} reshape(bf16[8,64,8,64]{3,2,1,0:T(8,128)(2,1)} %get-tuple-element.11) | data formatting | bytes 1048576 | tf_op jit(solution)/shard_map/jit(kron)/mul | solution.py:30
  20.8 2.6 %mul.403 = bf16[512,512]{1,0:T(8,128)(2,1)} reshape(bf16[8,64,8,64]{3,2,1,0:T(8,128)(2,1)} %get-tuple-element.12) | data formatting | bytes 1048576 | tf_op jit(solution)/shard_map/jit(kron)/mul | solution.py:30
  23.3 2.6 %mul.412 = bf16[512,512]{1,0:T(8,128)(2,1)} reshape(bf16[8,64,8,64]{3,2,1,0:T(8,128)(2,1)} %get-tuple-element.13) | data formatting | bytes 1048576 | tf_op jit(solution)/shard_map/jit(kron)/mul | solution.py:30
  25.9 2.6 %mul.398 = bf16[512,512]{1,0:T(8,128)(2,1)} reshape(bf16[8,64,8,64]{3,2,1,0:T(8,128)(2,1)} %get-tuple-element.14) | data formatting | bytes 1048576 | tf_op jit(solution)/shard_map/jit(kron)/mul | solution.py:30
  28.4 2.6 %mul.410 = bf16[512,512]{1,0:T(8,128)(2,1)} reshape(bf16[8,64,8,64]{3,2,1,0:T(8,128)(2,1)} %get-tuple-element.15) | data formatting | bytes 1048576 | tf_op jit(solution)/shard_map/jit(kron)/mul | solution.py:30
  31.0 2.5 %mul.392 = bf16[512,512]{1,0:T(8,128)(2,1)} reshape(bf16[8,64,8,64]{3,2,1,0:T(8,128)(2,1)} %get-tuple-element.16) | data formatting | bytes 1048576 | tf_op jit(solution)/shard_map/jit(kron)/mul | solution.py:30
  33.5 1.4 mul.408
  35.0 0.0 copy-start.3
  35.0 1.2 bitcast_dynamic-update-slice_fusion.7
  36.2 1.1 bitcast_dynamic-update-slice_fusion.6
  37.3 1.1 bitcast_dynamic-update-slice_fusion.5
  38.5 1.1 bitcast_dynamic-update-slice_fusion.4
  39.6 0.0 copy-done.3
  39.6 0.1 bitcast_dynamic-update-slice_fusion.3
  39.6 0.0 copy-done.5
  39.7 0.1 bitcast_dynamic-update-slice_fusion.2
  39.7 0.0 copy-done.4
  39.7 0.1 bitcast_dynamic-update-slice_fusion.1
  39.8 0.0 copy-done.2
  39.8 0.1 bitcast_dynamic-update-slice_fusion
  39.9 1.4 fusion
  41.2 0.0 copy-start.6
  41.2 0.6 copy-done.6
  41.9 10.3 %all_gather.3 = bf16[128,512]{1,0:T(8,128)(2,1)S(1)} all-gather(bf16[32,512]{1,0:T(8,128)(2,1)S(1)} %fusion), channel_id=1, replica_groups=mesh['slab'=128,'sub'=4] {'sub'}, dimensions={0}, use_global_device_ids=true | all-gather | bytes 163840 | tf_op jit(solution)/shard_map/all_gather | solution.py:40
  52.1 4.0 %gather_fusion = bf16[1024,512]{1,0:T(8,128)(2,1)S(1)} fusion(bf16[128,512]{1,0:T(8,128)(2,1)S(1)} %all_gather.3, s32[1024]{0:T(1024)S(1)} %broadcast_clamp_fusion), kind=kCustom, calls=%fused_computation | custom fusion | bytes 2101248 | tf_op jit(solution)/shard_map/jit(_take)/gather | solution.py:42
  56.1 0.0 copy-done.7
  56.1 0.0 copy-start.8
  56.1 0.0 copy-start.9
  56.1 0.0 copy-start.10
  56.1 1.2 bitcast_select_fusion
  57.3 20.5 %all-to-all-start = ((bf16[128,8,512]{2,1,0:T(8,128)(2,1)}), bf16[128,8,512]{2,1,0:T(8,128)(2,1)S(1)}, u32[]{:S(2)}, u32[]{:S(2)}) async-start(bf16[128,8,512]{2,1,0:T(8,128)(2,1)} %bitcast_select_fusion), calls=%async_computation | async-start | bytes 2097152 | tf_op jit(solution)/shard_map/all_to_all | solution.py:43
  77.8 0.0 reduce-scatter.2.cloned.1.call-start
  77.9 0.0 copy-done.8
  77.9 0.0 copy-done.9
  77.9 0.0 copy-done.10
  77.9 0.1 fusion.7
  78.0 30.2 %all-to-all-done = bf16[128,8,512]{2,1,0:T(8,128)(2,1)S(1)} async-done(((bf16[128,8,512]{2,1,0:T(8,128)(2,1)}), bf16[128,8,512]{2,1,0:T(8,128)(2,1)S(1)}, u32[]{:S(2)}, u32[]{:S(2)}) %all-to-all-start) | async-done | bytes 1048608 | tf_op jit(solution)/shard_map/all_to_all | solution.py:43
  108.3 1.0 copy-done.1
  109.2 1.3 pad_maximum_fusion
  110.5 2.6 %gather_fusion.1 = bf16[512,512]{1,0:T(8,128)(2,1)} fusion(bf16[1152,512]{1,0:T(8,128)(2,1)S(1)} %pad_maximum_fusion, s32[1024]{0:T(1024)S(1)} %pad_clamp_fusion), kind=kCustom, calls=%fused_computation.1 | custom fusion | bytes 1050624 | tf_op jit(solution)/shard_map/jit(_take)/gather | solution.py:46
  113.2 0.0 copy-done
  113.2 1.9 %convolution_multiply_fusion = f32[4,128,512]{2,1,0:T(8,128)S(1)} fusion(bf16[4,512,512]{2,1,0:T(8,128)(2,1)S(1)} %copy-done, f32[4,128]{1,0:T(4,128)S(1)} %get-tuple-element.27, bf16[4,128,512]{2,1,0:T(8,128)(2,1)} %bitcast.70, pred[4,128]{1,0:T(4,128)(4,1)S(1)} %get-tuple-element.28), kind=kOutput, calls=%fused_computation.11 | convolution fusion | flops 268959744 | bytes 3672576 | tf_op jit(solution)/shard_map/kcn,kmn->kcm/dot_general | solution.py:47
  115.0 3.6 %scatter_custom_fusion = f32[128,512]{1,0:T(8,128)S(1)} fusion(s32[512]{0:T(512)S(1)} %bitcast.73, f32[512,512]{1,0:T(8,128)S(1)} %bitcast.71, f32[]{:T(128)} %constant.27.clone.1), kind=kCustom, calls=%fused_computation.27 | custom fusion | flops 262144 | bytes 262148 | tf_op jit(solution)/shard_map/scatter-add | solution.py:51
  118.7 0.7 convert_element_type.23
  119.4 0.0 reduce-scatter.2.cloned.1.call-update
  119.4 17.0 %reduce-scatter.2.cloned.1.call-done = bf16[32,512]{1,0:T(8,128)(2,1)} async-done(((bf16[128,512]{1,0:T(8,128)(2,1)}), bf16[32,512]{1,0:T(8,128)(2,1)}) %reduce-scatter.2.cloned.1.call-update) | async-done | bytes 32784 | tf_op jit(solution)/shard_map/reduce_scatter | solution.py:52
  136.4 1.4 convert_element_type.24
  (13 shorter events, 0.1 us)
Async XLA Ops:
  7.2 106.0 %copy-start = (bf16[4,512,512]{2,1,0:T(8,128)(2,1)S(1)}, bf16[4,512,512]{2,1,0:T(8,128)(2,1)}, u32[]{:S(2)}) copy-start(bf16[4,512,512]{2,1,0:T(8,128)(2,1)} %param.7) | copy-start | bytes 6291460
  35.0 4.6 %copy-start.3 = (bf16[512,512]{1,0:T(8,128)(2,1)S(1)}, bf16[512,512]{1,0:T(8,128)(2,1)}, u32[]{:S(2)}) copy-start(bf16[512,512]{1,0:T(8,128)(2,1)} %mul.406) | copy-start | bytes 1572868
  35.0 4.7 %copy-start.5 = (bf16[512,512]{1,0:T(8,128)(2,1)S(1)}, bf16[512,512]{1,0:T(8,128)(2,1)}, u32[]{:S(2)}) copy-start(bf16[512,512]{1,0:T(8,128)(2,1)} %mul.408) | copy-start | bytes 1572868
  35.0 4.8 %copy-start.4 = (bf16[512,512]{1,0:T(8,128)(2,1)S(1)}, bf16[512,512]{1,0:T(8,128)(2,1)}, u32[]{:S(2)}) copy-start(bf16[512,512]{1,0:T(8,128)(2,1)} %mul.410) | copy-start | bytes 1572868
  35.0 4.8 %copy-start.2 = (bf16[512,512]{1,0:T(8,128)(2,1)S(1)}, bf16[512,512]{1,0:T(8,128)(2,1)}, u32[]{:S(2)}) copy-start(bf16[512,512]{1,0:T(8,128)(2,1)} %mul.412) | copy-start | bytes 1572868
  41.2 0.6 copy-start.6
  52.1 4.0 %copy-start.7 = (pred[128,8]{1,0:T(8,128)(4,1)S(1)}, pred[128,8]{1,0:T(8,128)(4,1)}, u32[]{:S(2)}) copy-start(pred[128,8]{1,0:T(8,128)(4,1)} %copy.11) | copy-start | bytes 3076
  56.1 21.8 %copy-start.8 = (s32[1,4,128]{2,1,0:T(4,128)S(1)}, s32[1,4,128]{2,1,0:T(4,128)}, u32[]{:S(2)}) copy-start(s32[1,4,128]{2,1,0:T(4,128)} %param.10) | copy-start | bytes 6148
  56.1 21.8 %copy-start.9 = (s32[1,4,128]{2,1,0:T(4,128)S(1)}, s32[1,4,128]{2,1,0:T(4,128)}, u32[]{:S(2)}) copy-start(s32[1,4,128]{2,1,0:T(4,128)} %param.9) | copy-start | bytes 6148
  56.1 21.8 %copy-start.10 = (s32[1,4]{1,0:T(1,128)S(1)}, s32[1,4]{1,0:T(1,128)}, u32[]{:S(2)}) copy-start(s32[1,4]{1,0:T(1,128)} %param.11) | copy-start | bytes 52
  57.3 50.9 %all-to-all-start = ((bf16[128,8,512]{2,1,0:T(8,128)(2,1)}), bf16[128,8,512]{2,1,0:T(8,128)(2,1)S(1)}, u32[]{:S(2)}, u32[]{:S(2)}) async-start(bf16[128,8,512]{2,1,0:T(8,128)(2,1)} %bitcast_select_fusion), calls=%async_computation | async-start | bytes 2097152 | tf_op jit(solution)/shard_map/all_to_all | solution.py:43
  77.8 58.6 %reduce-scatter.2.cloned.1.call-start = ((), (), s32[]{:S(2)}) async-start(), calls=%async_computation.2 | async-start | bytes 163840 | tf_op jit(solution)/shard_map/reduce_scatter | solution.py:52
  108.3 1.0 copy-start.1
Sparse Core Ops, SparseCore 0:
  119.5 16.8 reduce-scatter.1
where the time goes:
time: 147 us; the launch traced here: 145 us
  waiting for transfers between devices  47.3 us (32%)
  local copies, waits for them, and re-layouts  34.8 us (24%)
  starting transfers between devices  20.5 us (14%)
  between operations  14.3 us (10%)
  other arithmetic  14.2 us (10%)
  blocking collectives  10.3 us (7%)
  matrix products  3.23 us (2%)
    all_to_all x1, waiting for transfers between devices, body(): lax.all_to_all(picked, 'slab', split_axis=0, concat_axis=0, tiled=True)  30.2 us
    all_to_all x1, starting transfers between devices, body(): lax.all_to_all(picked, 'slab', split_axis=0, concat_axis=0, tiled=True)  20.5 us
    mul x12, local copies, waits for them, and re-layouts, upward_matrix(): blocks.append(jnp.kron(first, jnp.kron(second, third)).T)  19.8 us
    reduce_scatter x1, waiting for transfers between devices, body(): lax.psum_scatter(total.astype(jnp.bfloat16), 'sub', scatter_dimension=0,...  17 us
    all_gather x1, blocking collectives, body(): segment = lax.all_gather(parents, 'sub', axis=0, tiled=True)  10.3 us
    unnamed x29, local copies, waits for them, and re-layouts  6.39 us
    gather x1, local copies, waits for them, and re-layouts, body(): picked = jnp.take(segment, send_index[0], axis=0)  3.96 us
    another operation x1, other arithmetic  3.94 us
  transfers between devices with their start and end apart: 2, of which 2 were waited for; matrix products, arithmetic and copies ran while one was open for 0% of the time, Pallas kernels for 0%

commit v1 on v0

v1 whole, which is shorter than its diff:
```python
import functools
import math

import jax
import jax.numpy as jnp
import numpy as np
from jax import lax
from jax.experimental import pallas as pl
from jax.experimental.pallas import tpu as pltpu
from jax.sharding import Mesh, PartitionSpec as P

ORDER = 8
NODES = 512
SEG = 128
GHOST = 8
TABLE = 1152
BASE = 32
CHIPS = 64
SUBS = 4
PEERS = 8
ROWS = 32
MSG = 48
EIGHTH = 64
LANES = 128
WIDTH = 384
PLAN_FLOPS = 1 << 34
VMEM = 60 << 20
SMALL_VMEM = 16 << 20
BF = jnp.bfloat16
F32 = jnp.float32


def one_side(side):
    counter = np.arange(ORDER, dtype=np.float32)
    angles = (np.float32(2.0) * counter + np.float32(1.0)) * np.float32(math.pi) / np.float32(2.0 * ORDER)
    nodes = np.cos(angles)
    degree = np.arange(1, ORDER, dtype=np.float32)
    parent_poly = np.cos(degree[:, None] * angles[None, :])
    child_pts = (nodes + np.float32(2.0 * side - 1.0)) / np.float32(2.0)
    child_poly = np.cos(degree[:, None] * np.arccos(child_pts)[None, :])
    summed = np.sum(parent_poly[:, :, None] * child_poly[:, None, :], axis=0)
    return (np.float32(1.0 / ORDER) + np.float32(2.0 / ORDER) * summed).astype(np.float32)


def upward_matrix():
    sides = [one_side(0), one_side(1)]
    blocks = []
    for octant in range(8):
        first = sides[octant >> 2 & 1]
        second = sides[octant >> 1 & 1]
        third = sides[octant & 1]
        blocks.append(np.kron(first, np.kron(second, third)).T)
    return np.stack(blocks).astype(BF)


def dot(a, b):
    return lax.dot_general(a, b, (((1,), (0,)), ((), ())), preferred_element_type=F32)


def dot_t(a, b):
    return lax.dot_general(a, b, (((1,), (1,)), ((), ())), preferred_element_type=F32)


def iota(shape, axis):
    return lax.broadcasted_iota(jnp.int32, shape, axis)


def onehot(flags):
    return jnp.where(flags, 1.0, 0.0).astype(BF)


def upward_kernel(
    count_hbm, leaves_hbm, target_hbm, source_hbm, send_hbm, weights_hbm, ops_hbm,
    parents_ref, msg_ref, own_ref, side_ref, across_ref,
    count_ref, leaves_ref, target_ref, source_ref, send_ref, w_ref, ops_ref, sems,
):
    sub, core = lax.axis_index("x"), lax.axis_index("c")
    pairs = ((count_hbm, count_ref), (target_hbm, target_ref), (source_hbm, source_ref), (send_hbm, send_ref), (leaves_hbm, leaves_ref))
    copies = [pltpu.make_async_copy(source, to, sems.at[i]) for i, (source, to) in enumerate(pairs)]
    copies += [pltpu.make_async_copy(ops_hbm.at[k], ops_ref.at[k], sems.at[5 + k]) for k in range(4)]
    copies += [pltpu.make_async_copy(weights_hbm.at[c], w_ref.at[c], sems.at[9 + c]) for c in range(8)]
    for copy in copies:
        copy.start()
    for copy in copies[:4]:
        copy.wait()
    slot = iota((1, SEG), 1)
    row = iota((8, SEG), 0)
    info = jnp.zeros((8, SEG), F32)
    for k in range(4):
        live = slot < count_ref[0:1, k : k + 1]
        target = jnp.where(live, target_ref[0, k : k + 1, :], -1)
        source = source_ref[0, k : k + 1, :]
        match = onehot(iota((SEG, SEG), 0) == target)
        high = jnp.where(live, (source >> 5) + 1, 0).astype(F32)
        low = jnp.where(live, source & (BASE - 1), 0).astype(F32)
        info = info + dot_t(jnp.where(row == k, high, jnp.where(row == 4 + k, low, 0.0)).astype(BF), match)
    tail = jnp.concatenate([send_ref[...].astype(F32), info], axis=0).astype(BF)
    for e in range(PEERS):
        msg_ref[e, ROWS:MSG, :] = tail
    to, at = iota((256, 256), 0), iota((256, 256), 1)
    sort = onehot(at == (to & 31) * 8 + (to >> 5))
    copies[4].wait()
    sorted_leaves = dot(sort, leaves_ref[...]).astype(BF)
    for copy in copies[5:9]:
        copy.wait()
    to, at = iota((4 * EIGHTH, 4 * LANES), 0), iota((4 * EIGHTH, 4 * LANES), 1)

    def columns(c, x):
        start = pl.multiple_of((2 * c + (x >> 1)) * LANES, LANES)
        tiles = jnp.concatenate([ops_ref[k, :, pl.ds(start, LANES)] for k in range(4)], axis=1)
        pick = onehot(at == (to >> 6) * LANES + (x & 1) * EIGHTH + (to & (EIGHTH - 1)))
        return dot_t(pick, tiles).astype(BF)

    beside = (sub + 3 + 2 * core) & 3
    across_ref[...] = columns(core, (sub + 2) & 3)
    side_ref[0] = columns(core, beside)
    side_ref[1] = columns(1 - core, beside)
    own_ref[...] = columns(core, sub)
    total = jnp.zeros((ROWS, NODES), F32)
    for c in range(8):
        copies[9 + c].wait()
        total = total + dot(sorted_leaves[c * ROWS : (c + 1) * ROWS, :], w_ref[c])
    parents = total.astype(BF)
    parents_ref[...] = parents
    wide = parents.astype(F32)
    lane = iota((ROWS, LANES), 1)
    for j in range(4):
        block = wide[:, j * LANES : (j + 1) * LANES]
        turned = pltpu.roll(block, EIGHTH, 1)
        msg_ref[2 * j, 0:ROWS, :] = jnp.where(lane < EIGHTH, block, turned).astype(BF)
        msg_ref[2 * j + 1, 0:ROWS, :] = jnp.where(lane < EIGHTH, turned, block).astype(BF)


def upward(leaves, target, source, count, send, weights, ops):
    vmem = pl.BlockSpec(memory_space=pltpu.VMEM)
    return pl.pallas_call(
        upward_kernel,
        out_shape=(jax.ShapeDtypeStruct((ROWS, NODES), BF), jax.ShapeDtypeStruct((PEERS, MSG, LANES), BF))
        + tuple(jax.ShapeDtypeStruct(shape + (4 * EIGHTH, NODES), BF) for shape in ((), (2,), ())),
        in_specs=[pl.BlockSpec(memory_space=pl.ANY)] * 7,
        out_specs=(vmem,) * 5,
        scratch_shapes=[
            pltpu.VMEM((1, 4), jnp.int32),
            pltpu.VMEM((256, NODES), BF),
            pltpu.VMEM((1, 4, SEG), jnp.int32),
            pltpu.VMEM((1, 4, SEG), jnp.int32),
            pltpu.VMEM((GHOST, SEG), jnp.int32),
            pltpu.VMEM((8, NODES, NODES), BF),
            pltpu.VMEM((4, NODES, NODES), BF),
            pltpu.SemaphoreType.DMA((17,)),
        ],
        compiler_params=pltpu.CompilerParams(vmem_limit_bytes=VMEM),
        cost_estimate=pl.CostEstimate(flops=2 * 256 * 512 * 512, bytes_accessed=5 << 20, transcendentals=0),
        name="upward",
    )(count, leaves, target, source, send, weights, ops)


def pick_kernel(got_ref, out_ref):
    parents = jnp.concatenate([got_ref[j, 0:ROWS, :] for j in range(PEERS)], axis=0)
    lane = iota((2 * SEG, LANES), 1)
    zero = jnp.zeros_like(parents)
    rhs = jnp.concatenate([jnp.where(lane < EIGHTH, parents, zero), jnp.where(lane < EIGHTH, zero, parents)], axis=0)
    send = jnp.concatenate([got_ref[0, ROWS : ROWS + 8, :].astype(F32), got_ref[4, ROWS : ROWS + 8, :].astype(F32) + SEG], axis=0)
    send = send.astype(jnp.int32)
    at = iota((16, 2 * SEG), 1)
    step = 16
    for first in range(0, CHIPS, step):
        blocks = []
        for d in range(first, first + step):
            halves = [onehot(send[:, 2 * d + h : 2 * d + h + 1] == at) for h in range(2)]
            blocks.append(jnp.concatenate(halves, axis=1))
        lhs = jnp.concatenate(blocks, axis=0)
        out_ref[first * 16 : (first + step) * 16, :] = dot(lhs, rhs).astype(BF)


def pick(got):
    vmem = pl.BlockSpec(memory_space=pltpu.VMEM)
    return pl.pallas_call(
        pick_kernel,
        out_shape=jax.ShapeDtypeStruct((CHIPS * 16, LANES), BF),
        in_specs=[vmem],
        out_specs=vmem,
        compiler_params=pltpu.CompilerParams(vmem_limit_bytes=SMALL_VMEM),
        cost_estimate=pl.CostEstimate(flops=PLAN_FLOPS, bytes_accessed=1 << 19, transcendentals=0),
        name="pick",
    )(got)


def plan_kernel(got_ref, early_ref, late_ref, out_ref):
    sub, core = lax.axis_index("x"), lax.axis_index("c")
    groups = (sub, sub + 1 + 2 * core, sub + 2, sub + 3 + 2 * core)
    for q in range(2):
        for d in range(SUBS):
            info = got_ref[q * 4 + (groups[d] & 3), ROWS + 8 : MSG, :].astype(F32)
            source = ((info[0:4, :] - 1.0) * BASE + info[4:8, :]).astype(jnp.int32)
            ghost = source - SEG
            at = q * 16 + d * 4
            out_ref[at : at + 4, :] = jnp.where(source < SEG, jnp.where(source < 0, -1, source + 256), ghost & 255)
            out_ref[32 + at : 36 + at, :] = jnp.where(source < SEG, 0, ghost >> 8)


def plan(got, early, late):
    vmem = pl.BlockSpec(memory_space=pltpu.VMEM)
    return pl.pallas_call(
        plan_kernel,
        out_shape=jax.ShapeDtypeStruct((64, SEG), jnp.int32),
        in_specs=[vmem] + [pl.BlockSpec(memory_space=pl.ANY)] * 2,
        out_specs=vmem,
        compiler_params=pltpu.CompilerParams(vmem_limit_bytes=SMALL_VMEM),
        cost_estimate=pl.CostEstimate(flops=PLAN_FLOPS, bytes_accessed=5 << 20, transcendentals=0),
        name="plan",
    )(got, early, late)


def local_kernel(got_ref, ghosts_ref, plan_ref, m0_hbm, m1_hbm, m2_hbm, m3_hbm, out_ref, m_ref, rows_ref, rhs_ref, x_ref, sems):
    sources = (m0_hbm, m1_hbm.at[0], m2_hbm, m3_hbm)
    copies = [pltpu.make_async_copy(m, m_ref.at[d], sems.at[d]) for d, m in enumerate(sources)]
    for copy in copies:
        copy.start()
    row = iota((WIDTH, SEG), 0)
    for q in range(2):
        for k in range(16):
            at = q * 16 + k
            rows_ref[q, :, k * SEG : (k + 1) * SEG] = onehot(plan_ref[at : at + 1, :] == row)
    for q in range(2):
        own = jnp.concatenate([got_ref[q * 4 + j, 0:ROWS, 0:EIGHTH] for j in range(4)], axis=0).astype(F32).T
        rhs_ref[q, 0:EIGHTH, 256:WIDTH] = own.astype(BF)
        rhs_ref[q, EIGHTH:256, 256:WIDTH] = jnp.zeros((256 - EIGHTH, SEG), BF)
    for b in range(4):
        block = ghosts_ref[b * 256 : (b + 1) * 256, :].astype(F32).T.astype(BF)
        rhs_ref[0, b * EIGHTH : (b + 1) * EIGHTH, 0:256] = block[0:EIGHTH, :]
        rhs_ref[1, b * EIGHTH : (b + 1) * EIGHTH, 0:256] = block[EIGHTH:LANES, :]
    for q in range(2):
        for k in range(0, 16, 2):
            both = dot(rhs_ref[q], rows_ref[q, :, k * SEG : (k + 2) * SEG])
            for i in range(k, k + 2):
                at = 32 + q * 16 + i
                block = plan_ref[at : at + 1, :]
                part = both[:, (i - k) * SEG : (i - k + 1) * SEG]
                kept = jnp.where(block == 0, part[0:EIGHTH, :], 0.0)
                for b in range(1, 4):
                    kept = jnp.where(block == b, part[b * EIGHTH : (b + 1) * EIGHTH, :], kept)
                x_ref[i * EIGHTH : (i + 1) * EIGHTH, q * SEG : (q + 1) * SEG] = kept.astype(BF)
    for copy in copies:
        copy.wait()
    total = lax.dot_general(x_ref[...], m_ref[...].reshape(1024, NODES), (((0,), (0,)), ((), ())), preferred_element_type=F32)
    out_ref[...] = total.astype(BF)


def local_sums(got, ghosts, columns, ops):
    vmem, anywhere = pl.BlockSpec(memory_space=pltpu.VMEM), pl.BlockSpec(memory_space=pl.ANY)
    return pl.pallas_call(
        local_kernel,
        out_shape=jax.ShapeDtypeStruct((2 * SEG, NODES), BF),
        in_specs=[vmem] * 3 + [anywhere] * 4,
        out_specs=vmem,
        scratch_shapes=[
            pltpu.VMEM((SUBS, 256, NODES), BF),
            pltpu.VMEM((2, WIDTH, 16 * SEG), BF),
            pltpu.VMEM((2, 256, WIDTH), BF),
            pltpu.VMEM((1024, 2 * SEG), BF),
            pltpu.SemaphoreType.DMA((4,)),
        ],
        compiler_params=pltpu.CompilerParams(vmem_limit_bytes=SMALL_VMEM),
        cost_estimate=pl.CostEstimate(flops=2 * 4096 * 512 * 256, bytes_accessed=5 << 20, transcendentals=0),
        name="local_sums",
    )(got, ghosts, columns, *ops)


def body(weights, leaves, m2l_ops, send_index, pair_target, pair_source, pair_count):
    send = jnp.transpose(send_index, (0, 2, 1)).reshape(GHOST, SEG)
    parents, message, own, side, across = upward(leaves, pair_target, pair_source, pair_count, send, weights, m2l_ops)
    got = lax.all_to_all(message, ("c", "x"), 0, 0, tiled=True)
    across = lax.ppermute(across, "x", [(i, (i + 2) % SUBS) for i in range(SUBS)])
    steps = [(c * SUBS + i, c * SUBS + (i + 3 + 2 * c) % SUBS) for c in range(2) for i in range(SUBS)]
    side = lax.ppermute(side, ("c", "x"), steps)
    swapped = lax.ppermute(side[1], "c", [(0, 1), (1, 0)])
    ghosts = lax.all_to_all(pick(got), ("y", "z"), 0, 0, tiled=True)
    columns = plan(got, side, across)
    ops = (own, side, across, swapped)
    sums = local_sums(got, ghosts, columns, ops)
    parts = lax.all_to_all(sums, ("c", "x"), 0, 0, tiled=True)
    local = jnp.sum(parts.reshape(PEERS, ROWS, NODES).astype(F32), axis=0)
    return (parents, local)


def solution(mesh):
    four = Mesh(mesh.devices.reshape(8, 8, 2, SUBS), ("y", "z", "c", "x"))
    slab = ("y", "z", "c")
    every = slab + ("x",)
    in_specs = (
        P(every, None),
        P("x", None, None),
        P(slab, None, None),
        P(slab, "x", None),
        P(slab, "x", None),
        P(slab, "x"),
    )
    out_specs = (P(every, None), P(every, None))
    weights = upward_matrix()
    return jax.shard_map(
        lambda *args: body(jnp.asarray(weights), *args), mesh=four, in_specs=in_specs, out_specs=out_specs, check_vma=False
    )
```

time: 147 us -> 64.4 us (0.44); the launches traced: 145 us -> 64 us
  waiting for transfers between devices: 47.3 us -> 8.54 us
  local copies, waits for them, and re-layouts: 34.8 us -> 0.02 us
  between operations: 14.3 us -> 0.73 us
  other arithmetic: 14.2 us -> 0.67 us
  starting transfers between devices: 20.5 us -> 32.9 us
  Pallas kernels: 0 us -> 7.92 us
  matrix products: 3.23 us -> 0 us
  blocking collectives: 10.3 us -> 13.2 us
    all_to_all x1 -> x2, waiting for transfers between devices: 30.2 us -> 8.53 us  [the longest x1 8.53 us: body(): ghosts = lax.all_to_all(pick(got), ('y', 'z'), 0, 0, tiled=True)]
    mul x12 -> x0, local copies, waits for them, and re-layouts: 19.8 us -> none  [upward_matrix(): blocks.append(jnp.kron(first, jnp.kron(second, third)).T)]
    reduce_scatter x1 -> x0, waiting for transfers between devices: 17 us -> none  [body(): lax.psum_scatter(total.astype(jnp.bfloat16), 'sub', scatter_dimension=0,...]
    all_to_all x0 -> x1, blocking collectives: none -> 13.2 us  [body(): parts = lax.all_to_all(sums, ('c', 'x'), 0, 0, tiled=True)]
    ppermute x0 -> x3, starting transfers between devices: none -> 10.8 us  [the longest x1 4.78 us: body(): lax.ppermute(across, 'x', [(i, (i + 2) % SUBS) for i in range(SUBS)])]
    all_gather x1 -> x0, blocking collectives: 10.3 us -> none  [body(): segment = lax.all_gather(parents, 'sub', axis=0, tiled=True)]
    pallas_call x0 -> x4, Pallas kernels: none -> 7.92 us  [the longest x1 4.3 us: upward(): pl.pallas_call(upward_kernel, out_shape=(jax.ShapeDtypeStruct((ROWS, NODE...]
    gather x2 -> x0, local copies, waits for them, and re-layouts: 6.59 us -> none  [the longest x1 3.96 us: body(): picked = jnp.take(segment, send_index[0], axis=0)]
  transfers between devices with their start and end apart: 2 -> 5, of which waited for: 2 -> 1; matrix products, arithmetic and copies ran while one was open for 0% -> 0% of each run, Pallas kernels for 0% -> 2%
where the time goes in v1:
time: 64.4 us; the launch traced here: 64 us
  starting transfers between devices  32.9 us (51%)
  blocking collectives  13.2 us (20%)
  waiting for transfers between devices  8.54 us (13%)
  Pallas kernels  7.92 us (12%)
  between operations  0.73 us (1%)
  other arithmetic  0.67 us (1%)
    all_to_all x1, blocking collectives, body(): parts = lax.all_to_all(sums, ('c', 'x'), 0, 0, tiled=True)  13.2 us
    all_to_all x1, starting transfers between devices, body(): ghosts = lax.all_to_all(pick(got), ('y', 'z'), 0, 0, tiled=True)  11.9 us
    all_to_all x1, starting transfers between devices, body(): got = lax.all_to_all(message, ('c', 'x'), 0, 0, tiled=True)  10.2 us
    all_to_all x1, waiting for transfers between devices, body(): ghosts = lax.all_to_all(pick(got), ('y', 'z'), 0, 0, tiled=True)  8.53 us
    ppermute x1, starting transfers between devices, body(): lax.ppermute(across, 'x', [(i, (i + 2) % SUBS) for i in range(SUBS)])  4.78 us
    pallas_call x1, Pallas kernels, upward(): pl.pallas_call(upward_kernel, out_shape=(jax.ShapeDtypeStruct((ROWS, NODE...  4.3 us
    ppermute x1, starting transfers between devices, body(): swapped = lax.ppermute(side[1], 'c', [(0, 1), (1, 0)])  3.84 us
    pallas_call x1, Pallas kernels, local_sums(): pl.pallas_call(local_kernel, out_shape=jax.ShapeDtypeStruct((2 * SEG, NOD...  2.25 us
  transfers between devices with their start and end apart: 5, of which 1 were waited for; matrix products, arithmetic and copies ran while one was open for 0% of the time, Pallas kernels for 2%

profile of v1, /device:TPU:1, one launch (start us, length us, event | category | flops | bytes accessed | tf_op | source)
XLA Modules:
  0.0 64.0 jit_solution(141619317228689638)
XLA Ops:
  0.6 4.3 %upward.1 = (bf16[32,512]{1,0:T(8,128)(2,1)}, bf16[8,48,128]{2,1,0:T(8,128)(2,1)}, bf16[256,512]{1,0:T(8,128)(2,1)}, bf16[2,256,512]{2,1,0:T(8,128)(2,1)}, bf16[256,512]{1,0:T(8,128)(2,1)}) custom-call(s32[1,4]{1,0:T(1,128)} %count_hbm.1, bf16[256,512]{1,0:T(8,128)(2,1)} %leaves_hbm.1, s32[1,4,128]{2,1,0:T(4,128)} %target_hbm.1, s32[1,4,128]{2,1,0:T(4,128)} %source_hbm.1, ...), custom_call_target="tpu_custom_call" | custom-call | flops 134217728 | bytes 5242880 | tf_op jit(solution)/shard_map/upward/pallas_call | solution.py:136
  4.9 10.2 %all-to-all-start = ((bf16[8,48,128]{2,1,0:T(8,128)(2,1)}), bf16[8,48,128]{2,1,0:T(8,128)(2,1)S(1)}, u32[]{:S(2)}, u32[]{:S(2)}) async-start(bf16[8,48,128]{2,1,0:T(8,128)(2,1)} %get-tuple-element.8), calls=%async_computation | async-start | bytes 196608 | tf_op jit(solution)/shard_map/all_to_all | solution.py:273
  15.1 4.8 %collective-permute-start.1 = (bf16[256,512]{1,0:T(8,128)(2,1)}, bf16[256,512]{1,0:T(8,128)(2,1)S(1)}, u32[]{:S(2)}, u32[]{:S(2)}) collective-permute-start(bf16[256,512]{1,0:T(8,128)(2,1)} %get-tuple-element.10), channel_id=1, source_target_pairs={{0,2},{1,3},{2,0},{3,1},{4,6},{5,7},{6,4},{7,5},{8,10},{9,11},{10,... | collective-permute-start | bytes 786440 | tf_op jit(solution)/shard_map/ppermute | solution.py:274
  19.9 2.2 %collective-permute-start = (bf16[2,256,512]{2,1,0:T(8,128)(2,1)}, bf16[2,256,512]{2,1,0:T(8,128)(2,1)S(1)}, u32[]{:S(2)}, u32[]{:S(2)}) collective-permute-start(bf16[2,256,512]{2,1,0:T(8,128)(2,1)} %get-tuple-element.9), channel_id=1, source_target_pairs={{0,3},{1,0},{2,1},{3,2},{4,5},{5,6},{6,7},{7,4},{8,11},{9,8},{10,9... | collective-permute-start | bytes 1572872 | tf_op jit(solution)/shard_map/ppermute | solution.py:276
  22.1 0.0 all-to-all-done.got_ref
  22.1 1.3 %pick.1 = bf16[1024,128]{1,0:T(8,128)(2,1)} custom-call(bf16[8,48,128]{2,1,0:T(8,128)(2,1)S(1)} %all-to-all-done.got_ref), custom_call_target="tpu_custom_call" | custom-call | flops 17179869184 | bytes 524288 | tf_op jit(solution)/shard_map/pick/pallas_call | solution.py:178
  23.5 11.9 %all-to-all-start.1 = ((bf16[64,16,128]{2,1,0:T(8,128)(2,1)}), bf16[64,16,128]{2,1,0:T(8,128)(2,1)S(1)}, u32[]{:S(2)}, u32[]{:S(2)}) async-start(bf16[64,16,128]{2,1,0:T(8,128)(2,1)} %bitcast.2), calls=%async_computation.1 | async-start | bytes 524288 | tf_op jit(solution)/shard_map/all_to_all | solution.py:278
  35.4 0.0 collective-permute-done.early_ref.m1_hbm
  35.5 0.0 copy-start
  35.5 3.8 %collective-permute-start.2 = (bf16[256,512]{1,0:T(8,128)(2,1)S(1)}, bf16[256,512]{1,0:T(8,128)(2,1)S(1)}, u32[]{:S(2)}, u32[]{:S(2)}) collective-permute-start(bf16[256,512]{1,0:T(8,128)(2,1)S(1)} %slice_bitcast_fusion), channel_id=1, source_target_pairs={{0,4},{4,0},{1,5},{5,1},{2,6},{6,2},{3,7},{7,3},{8,12},{12,8},{9,1... | collective-permute-start | bytes 786440 | tf_op jit(solution)/shard_map/ppermute | solution.py:277
  39.3 0.0 collective-permute-done.1.late_ref.m2_hbm
  39.4 8.5 %all-to-all-done.1 = bf16[64,16,128]{2,1,0:T(8,128)(2,1)S(1)} async-done(((bf16[64,16,128]{2,1,0:T(8,128)(2,1)}), bf16[64,16,128]{2,1,0:T(8,128)(2,1)S(1)}, u32[]{:S(2)}, u32[]{:S(2)}) %all-to-all-start.1) | async-done | bytes 262176 | tf_op jit(solution)/shard_map/all_to_all | solution.py:278
  47.9 0.0 collective-permute-done.2.m3_hbm
  47.9 0.0 copy-done
  47.9 2.2 %local_sums.1 = bf16[256,512]{1,0:T(8,128)(2,1)S(1)} custom-call(bf16[8,48,128]{2,1,0:T(8,128)(2,1)S(1)} %all-to-all-done.got_ref, bf16[1024,128]{1,0:T(8,128)(2,1)S(1)} %bitcast.8, s32[64,128]{1,0:T(8,128)S(1)} %plan.1.plan_ref, bf16[256,512]{1,0:T(8,128)(2,1)S(1)} %copy-done, bf16[2,256,512]{2,1,0:T(8,128)(2,1)S(1)} %collective-permute-done.early_ref.m1_hbm, ...), custom_call_target="tpu_custom_call" | custom-call | flops 1073741824 | bytes 5242880 | tf_op jit(solution)/shard_map/local_sums/pallas_call | solution.py:252
  50.1 13.2 %all_to_all.25 = bf16[8,32,512]{2,1,0:T(8,128)(2,1)S(1)} all-to-all(bf16[8,32,512]{2,1,0:T(8,128)(2,1)S(1)} %bitcast.9), channel_id=1, replica_groups=mesh['y'=8,'z'=8,'c'=2,'x'=4] {'c','x'}, dimensions={0} | all-to-all | bytes 524288 | tf_op jit(solution)/shard_map/all_to_all | solution.py:282
  63.3 0.7 %convert_reduce_fusion = f32[32,512]{1,0:T(8,128)} fusion(bf16[8,32,512]{2,1,0:T(8,128)(2,1)S(1)} %all_to_all.25), kind=kLoop, calls=%fused_computation | loop fusion | flops 245760 | bytes 327680 | tf_op jit(solution)/shard_map/reduce_sum | solution.py:283
  (2 shorter events, 0.1 us)
Async XLA Ops:
  4.9 17.2 %all-to-all-start = ((bf16[8,48,128]{2,1,0:T(8,128)(2,1)}), bf16[8,48,128]{2,1,0:T(8,128)(2,1)S(1)}, u32[]{:S(2)}, u32[]{:S(2)}) async-start(bf16[8,48,128]{2,1,0:T(8,128)(2,1)} %get-tuple-element.8), calls=%async_computation | async-start | bytes 196608 | tf_op jit(solution)/shard_map/all_to_all | solution.py:273
  15.1 24.2 %collective-permute-start.1 = (bf16[256,512]{1,0:T(8,128)(2,1)}, bf16[256,512]{1,0:T(8,128)(2,1)S(1)}, u32[]{:S(2)}, u32[]{:S(2)}) collective-permute-start(bf16[256,512]{1,0:T(8,128)(2,1)} %get-tuple-element.10), channel_id=1, source_target_pairs={{0,2},{1,3},{2,0},{3,1},{4,6},{5,7},{6,4},{7,5},{8,10},{9,11},{10,... | collective-permute-start | bytes 786440 | tf_op jit(solution)/shard_map/ppermute | solution.py:274
  19.9 15.5 %collective-permute-start = (bf16[2,256,512]{2,1,0:T(8,128)(2,1)}, bf16[2,256,512]{2,1,0:T(8,128)(2,1)S(1)}, u32[]{:S(2)}, u32[]{:S(2)}) collective-permute-start(bf16[2,256,512]{2,1,0:T(8,128)(2,1)} %get-tuple-element.9), channel_id=1, source_target_pairs={{0,3},{1,0},{2,1},{3,2},{4,5},{5,6},{6,7},{7,4},{8,11},{9,8},{10,9... | collective-permute-start | bytes 1572872 | tf_op jit(solution)/shard_map/ppermute | solution.py:276
  23.5 24.4 %all-to-all-start.1 = ((bf16[64,16,128]{2,1,0:T(8,128)(2,1)}), bf16[64,16,128]{2,1,0:T(8,128)(2,1)S(1)}, u32[]{:S(2)}, u32[]{:S(2)}) async-start(bf16[64,16,128]{2,1,0:T(8,128)(2,1)} %bitcast.2), calls=%async_computation.1 | async-start | bytes 524288 | tf_op jit(solution)/shard_map/all_to_all | solution.py:278
  35.5 12.4 %copy-start = (bf16[256,512]{1,0:T(8,128)(2,1)S(1)}, bf16[256,512]{1,0:T(8,128)(2,1)}, u32[]{:S(2)}) copy-start(bf16[256,512]{1,0:T(8,128)(2,1)} %get-tuple-element.11.m0_hbm) | copy-start | bytes 786436
  35.5 12.4 %collective-permute-start.2 = (bf16[256,512]{1,0:T(8,128)(2,1)S(1)}, bf16[256,512]{1,0:T(8,128)(2,1)S(1)}, u32[]{:S(2)}, u32[]{:S(2)}) collective-permute-start(bf16[256,512]{1,0:T(8,128)(2,1)S(1)} %slice_bitcast_fusion), channel_id=1, source_target_pairs={{0,4},{4,0},{1,5},{5,1},{2,6},{6,2},{3,7},{7,3},{8,12},{12,8},{9,1... | collective-permute-start | bytes 786440 | tf_op jit(solution)/shard_map/ppermute | solution.py:277

commit v2 on v1

v2 whole, which is shorter than its diff:
```python
import functools
import math

import jax
import jax.numpy as jnp
import numpy as np
from jax import lax
from jax.experimental import pallas as pl
from jax.experimental.pallas import tpu as pltpu
from jax.sharding import Mesh, PartitionSpec as P

ORDER = 8
NODES = 512
SEG = 128
GHOST = 8
TABLE = 1152
BASE = 32
CHIPS = 64
SUBS = 4
PEERS = 8
ROWS = 32
MSG = 48
OURS, THEIRS = 640, 384
EIGHTH = 64
LANES = 128
WIDTH = 384
PLAN_FLOPS = 1 << 34
VMEM = 60 << 20
SMALL_VMEM = 16 << 20
BF = jnp.bfloat16
F32 = jnp.float32


def one_side(side):
    counter = np.arange(ORDER, dtype=np.float32)
    angles = (np.float32(2.0) * counter + np.float32(1.0)) * np.float32(math.pi) / np.float32(2.0 * ORDER)
    nodes = np.cos(angles)
    degree = np.arange(1, ORDER, dtype=np.float32)
    parent_poly = np.cos(degree[:, None] * angles[None, :])
    child_pts = (nodes + np.float32(2.0 * side - 1.0)) / np.float32(2.0)
    child_poly = np.cos(degree[:, None] * np.arccos(child_pts)[None, :])
    summed = np.sum(parent_poly[:, :, None] * child_poly[:, None, :], axis=0)
    return (np.float32(1.0 / ORDER) + np.float32(2.0 / ORDER) * summed).astype(np.float32)


def upward_factors():
    sides = [one_side(0), one_side(1)]
    inner = [np.kron(np.eye(2), np.kron(sides[i >> 1], sides[i & 1]).T) for i in range(4)]
    outer = [np.kron(side.T, np.eye(EIGHTH)) for side in sides]
    inner = np.concatenate(inner).astype(np.float32)
    high = inner.astype(BF)
    low = (inner - high.astype(np.float32)).astype(BF)
    return np.concatenate([high, low], axis=1), np.concatenate(outer).astype(BF)


def dot(a, b):
    return lax.dot_general(a, b, (((1,), (0,)), ((), ())), preferred_element_type=F32)


def dot_t(a, b):
    return lax.dot_general(a, b, (((1,), (1,)), ((), ())), preferred_element_type=F32)


def iota(shape, axis):
    return lax.broadcasted_iota(jnp.int32, shape, axis)


def onehot(flags):
    return jnp.where(flags, 1.0, 0.0).astype(BF)


def upward_kernel(
    count_hbm, leaves_hbm, target_hbm, source_hbm, send_hbm, inner_hbm, outer_hbm, ops_hbm,
    parents_ref, msg_ref, own_hbm, side_hbm, across_hbm,
    count_ref, leaves_ref, target_ref, source_ref, send_ref, inner_ref, outer_ref, own_ref, side_ref, across_ref, sems, out_sems,
):
    sub, core = lax.axis_index("x"), lax.axis_index("c")
    own, beside, across = [pl.multiple_of((x & 3) * LANES, LANES) for x in (sub, sub + 3 + 2 * core, sub + 2)]
    small = ((count_hbm, count_ref), (target_hbm, target_ref), (source_hbm, source_ref), (send_hbm, send_ref))
    copies = [pltpu.make_async_copy(source, to, sems.at[i]) for i, (source, to) in enumerate(small)]
    copies += [pltpu.make_async_copy(leaves_hbm, leaves_ref, sems.at[4])]
    copies += [pltpu.make_async_copy(inner_hbm, inner_ref, sems.at[5]), pltpu.make_async_copy(outer_hbm, outer_ref, sems.at[6])]
    for copy in copies:
        copy.start()
    into = [
        pltpu.make_async_copy(ops_hbm.at[:, :, pl.ds(beside, LANES)], side_ref, out_sems.at[0]),
        pltpu.make_async_copy(ops_hbm.at[pl.ds(2 * core, 2), :, pl.ds(across, LANES)], across_ref, out_sems.at[1]),
        pltpu.make_async_copy(ops_hbm.at[:, :, pl.ds(own, LANES)], own_ref, out_sems.at[2]),
    ]
    out = [
        pltpu.make_async_copy(side_ref, side_hbm, out_sems.at[3]),
        pltpu.make_async_copy(across_ref, across_hbm, out_sems.at[4]),
        pltpu.make_async_copy(own_ref, own_hbm, out_sems.at[5]),
    ]
    for copy in into:
        copy.start()
    to, at = iota((256, 256), 0), iota((256, 256), 1)
    sort = onehot(at == (to & 31) * 8 + (to >> 5))
    for copy in copies[:4]:
        copy.wait()
    slot = iota((1, SEG), 1)
    row = iota((8, SEG), 0)
    digits, matches = [], []
    for k in range(4):
        live = slot < count_ref[0:1, k : k + 1]
        target = jnp.where(live, target_ref[0, k : k + 1, :], -1)
        source = source_ref[0, k : k + 1, :]
        high = jnp.where(live, (source >> 5) + 1, 0).astype(F32)
        low = jnp.where(live, source & (BASE - 1), 0).astype(F32)
        digits.append(jnp.where(row == k, high, jnp.where(row == 4 + k, low, 0.0)).astype(BF))
        matches.append(onehot(iota((SEG, SEG), 0) == target))
    info = dot_t(jnp.concatenate(digits, axis=1), jnp.concatenate(matches, axis=1))
    tail = jnp.concatenate([send_ref[...].astype(F32), info], axis=0).astype(BF)
    for e in range(PEERS):
        msg_ref[e, ROWS:MSG, :] = tail
    for i in range(3):
        into[i].wait()
        out[i].start()
    copies[4].wait()
    sorted_leaves = dot(sort, leaves_ref[...]).astype(BF)
    copies[5].wait()
    lhs = []
    for x in range(2):
        for j in range(4):
            parts = [sorted_leaves[(4 * x + i) * ROWS : (4 * x + i + 1) * ROWS, j * LANES : (j + 1) * LANES] for i in range(4)]
            lhs.append(jnp.concatenate(parts, axis=1))
    both = dot(jnp.concatenate(lhs, axis=0), inner_ref[...])
    partial = both[:, 0:LANES] + both[:, LANES:]
    partial = jnp.concatenate([partial[i * ROWS : (i + 1) * ROWS, :] for i in range(8)], axis=1)
    high = partial.astype(BF)
    low = (partial - high.astype(F32)).astype(BF)
    copies[6].wait()
    total = dot(jnp.concatenate([high, low], axis=0), outer_ref[...])
    total = total[0:ROWS, :] + total[ROWS:, :]
    parents = total.astype(BF)
    parents_ref[...] = parents
    wide = parents.astype(F32)
    lane = iota((ROWS, LANES), 1)
    for j in range(SUBS):
        block = wide[:, j * LANES : (j + 1) * LANES]
        turned = pltpu.roll(block, EIGHTH, 1)
        msg_ref[j, 0:ROWS, :] = jnp.where(lane < EIGHTH, block, turned).astype(BF)
        msg_ref[SUBS + j, 0:ROWS, :] = jnp.where(lane < EIGHTH, turned, block).astype(BF)
    for copy in out:
        copy.wait()


def upward(leaves, target, source, count, send, factors, ops):
    vmem, anywhere = pl.BlockSpec(memory_space=pltpu.VMEM), pl.BlockSpec(memory_space=pl.ANY)
    return pl.pallas_call(
        upward_kernel,
        out_shape=(
            jax.ShapeDtypeStruct((ROWS, NODES), BF),
            jax.ShapeDtypeStruct((PEERS, MSG, LANES), BF),
            jax.ShapeDtypeStruct((4, NODES, LANES), BF),
            jax.ShapeDtypeStruct((4, NODES, LANES), BF),
            jax.ShapeDtypeStruct((2, NODES, LANES), BF),
        ),
        in_specs=[anywhere] * 8,
        out_specs=(vmem, vmem, anywhere, anywhere, anywhere),
        scratch_shapes=[
            pltpu.VMEM((1, 4), jnp.int32),
            pltpu.VMEM((256, NODES), BF),
            pltpu.VMEM((1, 4, SEG), jnp.int32),
            pltpu.VMEM((1, 4, SEG), jnp.int32),
            pltpu.VMEM((GHOST, SEG), jnp.int32),
            pltpu.VMEM((4 * LANES, 2 * LANES), BF),
            pltpu.VMEM((2 * NODES, NODES), BF),
            pltpu.VMEM((4, NODES, LANES), BF),
            pltpu.VMEM((4, NODES, LANES), BF),
            pltpu.VMEM((2, NODES, LANES), BF),
            pltpu.SemaphoreType.DMA((7,)),
            pltpu.SemaphoreType.DMA((6,)),
        ],
        compiler_params=pltpu.CompilerParams(vmem_limit_bytes=VMEM),
        cost_estimate=pl.CostEstimate(flops=2 * 256 * 512 * 512, bytes_accessed=5 << 20, transcendentals=0),
        name="upward",
    )(count, leaves, target, source, send, *factors, ops)


def pick_kernel(got_ref, out_ref):
    parents = jnp.concatenate([got_ref[j, 0:ROWS, :] for j in range(PEERS)], axis=0)
    lane = iota((2 * SEG, LANES), 1)
    zero = jnp.zeros_like(parents)
    rhs = jnp.concatenate([jnp.where(lane < EIGHTH, parents, zero), jnp.where(lane < EIGHTH, zero, parents)], axis=0)
    send = jnp.concatenate([got_ref[0, ROWS : ROWS + 8, :].astype(F32), got_ref[4, ROWS : ROWS + 8, :].astype(F32) + SEG], axis=0)
    send = send.astype(jnp.int32)
    at = iota((16, 2 * SEG), 1)
    step = 16
    for first in range(0, CHIPS, step):
        blocks = []
        for d in range(first, first + step):
            halves = [onehot(send[:, 2 * d + h : 2 * d + h + 1] == at) for h in range(2)]
            blocks.append(jnp.concatenate(halves, axis=1))
        lhs = jnp.concatenate(blocks, axis=0)
        out_ref[first * 16 : (first + step) * 16, :] = dot(lhs, rhs).astype(BF)


def pick(got):
    vmem = pl.BlockSpec(memory_space=pltpu.VMEM)
    return pl.pallas_call(
        pick_kernel,
        out_shape=jax.ShapeDtypeStruct((CHIPS * 16, LANES), BF),
        in_specs=[vmem],
        out_specs=vmem,
        compiler_params=pltpu.CompilerParams(vmem_limit_bytes=SMALL_VMEM),
        cost_estimate=pl.CostEstimate(flops=PLAN_FLOPS, bytes_accessed=1 << 19, transcendentals=0),
        name="pick",
    )(got)


def plan_kernel(got_ref, own_ref, side_ref, across_ref, out_ref, ours_ref, theirs_ref):
    sub, core = lax.axis_index("x"), lax.axis_index("c")
    beside = (sub + 1 + 2 * core, sub + 3 + 2 * core)
    for q in range(2):
        groups = []
        for x in (sub, beside[0], beside[1], sub + 2):
            info = got_ref[q * 4 + (x & 3), ROWS + 8 : MSG, :].astype(F32)
            groups.append(((info[0:4, :] - 1.0) * BASE + info[4:8, :]).astype(jnp.int32))
        first, last = groups[3][0:2, :], groups[3][2:4, :]
        here, there = jnp.where(core == 0, first, last), jnp.where(core == 0, last, first)
        at = q * 16
        for source in (groups[0], groups[1], here, groups[2], there):
            rows = source.shape[0]
            ghost = source - SEG
            out_ref[at : at + rows, :] = jnp.where(source < SEG, jnp.where(source < 0, -1, source + 256), ghost & 255)
            out_ref[32 + at : 32 + at + rows, :] = jnp.where(source < SEG, 0, ghost >> 8)
            at += rows
    to, at = iota((EIGHTH, LANES), 0), iota((EIGHTH, LANES), 1)
    mine, other = onehot(at == core * EIGHTH + to), onehot(at == (1 - core) * EIGHTH + to)
    for k in range(6):
        tile = side_ref[k] if k < 4 else across_ref[k - 4]
        theirs_ref[k * EIGHTH : (k + 1) * EIGHTH, :] = dot_t(other, tile).astype(BF)
        ours_ref[(4 + k) * EIGHTH : (5 + k) * EIGHTH, :] = dot_t(mine, tile).astype(BF)
    for k in range(4):
        ours_ref[k * EIGHTH : (k + 1) * EIGHTH, :] = dot_t(mine, own_ref[k]).astype(BF)


def plan(got, own, side, across):
    vmem, anywhere = pl.BlockSpec(memory_space=pltpu.VMEM), pl.BlockSpec(memory_space=pl.ANY)
    return pl.pallas_call(
        plan_kernel,
        out_shape=(
            jax.ShapeDtypeStruct((64, SEG), jnp.int32),
            jax.ShapeDtypeStruct((OURS, NODES), BF),
            jax.ShapeDtypeStruct((THEIRS, NODES), BF),
        ),
        in_specs=[vmem] * 4,
        out_specs=(vmem, vmem, vmem),
        compiler_params=pltpu.CompilerParams(vmem_limit_bytes=SMALL_VMEM),
        cost_estimate=pl.CostEstimate(flops=PLAN_FLOPS, bytes_accessed=5 << 20, transcendentals=0),
        name="plan",
    )(got, own, side, across)


def local_kernel(got_ref, ghosts_ref, plan_ref, ours_hbm, theirs_hbm, out_ref, m_ref, rows_ref, rhs_ref, x_ref, sems):
    copies = [
        pltpu.make_async_copy(ours_hbm, m_ref.at[0:OURS], sems.at[0]),
        pltpu.make_async_copy(theirs_hbm, m_ref.at[OURS:1024], sems.at[1]),
    ]
    for copy in copies:
        copy.start()
    row = iota((WIDTH, SEG), 0)
    for q in range(2):
        for k in range(16):
            at = q * 16 + k
            rows_ref[q, :, k * SEG : (k + 1) * SEG] = onehot(plan_ref[at : at + 1, :] == row)
    for q in range(2):
        own = jnp.concatenate([got_ref[q * 4 + j, 0:ROWS, 0:EIGHTH] for j in range(4)], axis=0).astype(F32).T
        rhs_ref[q, 0:EIGHTH, 256:WIDTH] = own.astype(BF)
        rhs_ref[q, EIGHTH:256, 256:WIDTH] = jnp.zeros((256 - EIGHTH, SEG), BF)
    for b in range(4):
        block = ghosts_ref[b * 256 : (b + 1) * 256, :].astype(F32).T.astype(BF)
        rhs_ref[0, b * EIGHTH : (b + 1) * EIGHTH, 0:256] = block[0:EIGHTH, :]
        rhs_ref[1, b * EIGHTH : (b + 1) * EIGHTH, 0:256] = block[EIGHTH:LANES, :]
    for q in range(2):
        for k in range(0, 16, 2):
            both = dot(rhs_ref[q], rows_ref[q, :, k * SEG : (k + 2) * SEG])
            for i in range(k, k + 2):
                at = 32 + q * 16 + i
                block = plan_ref[at : at + 1, :]
                part = both[:, (i - k) * SEG : (i - k + 1) * SEG]
                kept = jnp.where(block == 0, part[0:EIGHTH, :], 0.0)
                for b in range(1, 4):
                    kept = jnp.where(block == b, part[b * EIGHTH : (b + 1) * EIGHTH, :], kept)
                x_ref[i * EIGHTH : (i + 1) * EIGHTH, q * SEG : (q + 1) * SEG] = kept.astype(BF)
    for copy in copies:
        copy.wait()
    total = lax.dot_general(x_ref[...], m_ref[...], (((0,), (0,)), ((), ())), preferred_element_type=F32)
    out_ref[...] = total.astype(BF)


def local_sums(got, ghosts, columns, ours, theirs):
    vmem, anywhere = pl.BlockSpec(memory_space=pltpu.VMEM), pl.BlockSpec(memory_space=pl.ANY)
    return pl.pallas_call(
        local_kernel,
        out_shape=jax.ShapeDtypeStruct((2 * SEG, NODES), BF),
        in_specs=[vmem] * 3 + [anywhere] * 2,
        out_specs=vmem,
        scratch_shapes=[
            pltpu.VMEM((1024, NODES), BF),
            pltpu.VMEM((2, WIDTH, 16 * SEG), BF),
            pltpu.VMEM((2, 256, WIDTH), BF),
            pltpu.VMEM((1024, 2 * SEG), BF),
            pltpu.SemaphoreType.DMA((2,)),
        ],
        compiler_params=pltpu.CompilerParams(vmem_limit_bytes=SMALL_VMEM),
        cost_estimate=pl.CostEstimate(flops=2 * 4096 * 512 * 256, bytes_accessed=5 << 20, transcendentals=0),
        name="local_sums",
    )(got, ghosts, columns, ours, theirs)


def body(factors, leaves, m2l_ops, send_index, pair_target, pair_source, pair_count):
    send = jnp.transpose(send_index, (0, 2, 1)).reshape(GHOST, SEG)
    parents, message, own, side, across = upward(leaves, pair_target, pair_source, pair_count, send, factors, m2l_ops)
    got = lax.all_to_all(message, ("c", "x"), 0, 0, tiled=True)
    steps = [(c * SUBS + i, c * SUBS + (i + 3 + 2 * c) % SUBS) for c in range(2) for i in range(SUBS)]
    side = lax.ppermute(side, ("c", "x"), steps)
    across = lax.ppermute(across, "x", [(i, (i + 2) % SUBS) for i in range(SUBS)])
    ghosts = lax.all_to_all(pick(got), ("y", "z"), 0, 0, tiled=True)
    columns, ours, theirs = plan(got, own, side, across)
    theirs = lax.ppermute(theirs, "c", [(0, 1), (1, 0)])
    sums = local_sums(got, ghosts, columns, ours, theirs)
    parts = lax.all_to_all(sums, ("c", "x"), 0, 0, tiled=True)
    local = jnp.sum(parts.reshape(PEERS, ROWS, NODES).astype(F32), axis=0)
    return (parents, local)


def solution(mesh):
    four = Mesh(mesh.devices.reshape(8, 8, 2, SUBS), ("y", "z", "c", "x"))
    slab = ("y", "z", "c")
    every = slab + ("x",)
    in_specs = (
        P(every, None),
        P("x", None, None),
        P(slab, None, None),
        P(slab, "x", None),
        P(slab, "x", None),
        P(slab, "x"),
    )
    out_specs = (P(every, None), P(every, None))
    factors = upward_factors()
    return jax.shard_map(
        lambda *args: body([jnp.asarray(factor) for factor in factors], *args), mesh=four, in_specs=in_specs, out_specs=out_specs, check_vma=False
    )
```

time: 64.4 us -> 63.8 us (level)
  blocking collectives: 13.2 us -> 11.7 us
  waiting for transfers between devices: 8.54 us -> 9.74 us
    all_to_all x1, blocking collectives: 13.2 us -> 11.7 us  [body(): parts = lax.all_to_all(sums, ('c', 'x'), 0, 0, tiled=True)]
    ppermute x1, starting transfers between devices: 3.84 us -> 2.5 us  [body(): theirs = lax.ppermute(theirs, 'c', [(0, 1), (1, 0)])]
    all_to_all x1, waiting for transfers between devices: 8.53 us -> 9.73 us  [body(): ghosts = lax.all_to_all(pick(got), ('y', 'z'), 0, 0, tiled=True)]
    ppermute x1, starting transfers between devices: 2.2 us -> 3.27 us  [body(): side = lax.ppermute(side, ('c', 'x'), steps)]
    pallas_call x1, Pallas kernels: 0.03 us -> 0.84 us  [plan(): pl.pallas_call(plan_kernel, out_shape=(jax.ShapeDtypeStruct((64, SEG), jn...]
    pallas_call x1, Pallas kernels: 4.3 us -> 3.53 us  [upward(): pl.pallas_call(upward_kernel, out_shape=(jax.ShapeDtypeStruct((ROWS, NODE...]
  transfers between devices with their start and end apart: 5 -> 5, of which waited for: 1 -> 1; matrix products, arithmetic and copies ran while one was open for 0% -> 0% of each run, Pallas kernels for 2% -> 3%
where the time goes in v2:
time: 63.8 us; the launch traced here: 63.4 us
  starting transfers between devices  32.3 us (51%)
  blocking collectives  11.7 us (18%)
  waiting for transfers between devices  9.74 us (15%)
  Pallas kernels  8.22 us (13%)
  between operations  0.73 us (1%)
  other arithmetic  0.67 us (1%)
    all_to_all x1, starting transfers between devices, body(): ghosts = lax.all_to_all(pick(got), ('y', 'z'), 0, 0, tiled=True)  11.9 us
    all_to_all x1, blocking collectives, body(): parts = lax.all_to_all(sums, ('c', 'x'), 0, 0, tiled=True)  11.7 us
    all_to_all x1, starting transfers between devices, body(): got = lax.all_to_all(message, ('c', 'x'), 0, 0, tiled=True)  10.2 us
    all_to_all x1, waiting for transfers between devices, body(): ghosts = lax.all_to_all(pick(got), ('y', 'z'), 0, 0, tiled=True)  9.73 us
    ppermute x1, starting transfers between devices, body(): lax.ppermute(across, 'x', [(i, (i + 2) % SUBS) for i in range(SUBS)])  4.45 us
    pallas_call x1, Pallas kernels, upward(): pl.pallas_call(upward_kernel, out_shape=(jax.ShapeDtypeStruct((ROWS, NODE...  3.53 us
    ppermute x1, starting transfers between devices, body(): side = lax.ppermute(side, ('c', 'x'), steps)  3.27 us
    pallas_call x1, Pallas kernels, local_sums(): pl.pallas_call(local_kernel, out_shape=jax.ShapeDtypeStruct((2 * SEG, NOD...  2.52 us
  transfers between devices with their start and end apart: 5, of which 1 were waited for; matrix products, arithmetic and copies ran while one was open for 0% of the time, Pallas kernels for 3%

profile of v2, /device:TPU:1, one launch (start us, length us, event | category | flops | bytes accessed | tf_op | source)
XLA Modules:
  0.0 63.4 jit_solution(14505598125440009154)
XLA Ops:
  0.6 3.5 %upward.1 = (bf16[32,512]{1,0:T(8,128)(2,1)}, bf16[8,48,128]{2,1,0:T(8,128)(2,1)}, bf16[4,512,128]{2,1,0:T(8,128)(2,1)}, bf16[4,512,128]{2,1,0:T(8,128)(2,1)}, bf16[2,512,128]{2,1,0:T(8,128)(2,1)}) custom-call(s32[1,4]{1,0:T(1,128)} %count_hbm.1, bf16[256,512]{1,0:T(8,128)(2,1)} %leaves_hbm.1, s32[1,4,128]{2,1,0:T(4,128)} %target_hbm.1, ...), custom_call_target="tpu_custom_call" | custom-call | flops 134217728 | bytes 5242880 | tf_op jit(solution)/shard_map/upward/pallas_call | solution.py:150
  4.2 10.2 %all-to-all-start = ((bf16[8,48,128]{2,1,0:T(8,128)(2,1)}), bf16[8,48,128]{2,1,0:T(8,128)(2,1)S(1)}, u32[]{:S(2)}, u32[]{:S(2)}) async-start(bf16[8,48,128]{2,1,0:T(8,128)(2,1)} %get-tuple-element.11), calls=%async_computation | async-start | bytes 196608 | tf_op jit(solution)/shard_map/all_to_all | solution.py:316
  14.3 3.3 %collective-permute-start = (bf16[4,512,128]{2,1,0:T(8,128)(2,1)}, bf16[4,512,128]{2,1,0:T(8,128)(2,1)S(1)}, u32[]{:S(2)}, u32[]{:S(2)}) collective-permute-start(bf16[4,512,128]{2,1,0:T(8,128)(2,1)} %get-tuple-element.13), channel_id=1, source_target_pairs={{0,3},{1,0},{2,1},{3,2},{4,5},{5,6},{6,7},{7,4},{8,11},{9,8},{10,9... | collective-permute-start | bytes 1572872 | tf_op jit(solution)/shard_map/ppermute | solution.py:318
  17.6 0.0 copy-start
  17.6 4.4 %collective-permute-start.1 = (bf16[2,512,128]{2,1,0:T(8,128)(2,1)}, bf16[2,512,128]{2,1,0:T(8,128)(2,1)S(1)}, u32[]{:S(2)}, u32[]{:S(2)}) collective-permute-start(bf16[2,512,128]{2,1,0:T(8,128)(2,1)} %get-tuple-element.14), channel_id=1, source_target_pairs={{0,2},{1,3},{2,0},{3,1},{4,6},{5,7},{6,4},{7,5},{8,10},{9,11},{10,... | collective-permute-start | bytes 786440 | tf_op jit(solution)/shard_map/ppermute | solution.py:319
  22.1 0.0 all-to-all-done.got_ref
  22.1 1.3 %pick.1 = bf16[1024,128]{1,0:T(8,128)(2,1)} custom-call(bf16[8,48,128]{2,1,0:T(8,128)(2,1)S(1)} %all-to-all-done.got_ref), custom_call_target="tpu_custom_call" | custom-call | flops 17179869184 | bytes 524288 | tf_op jit(solution)/shard_map/pick/pallas_call | solution.py:201
  23.4 11.9 %all-to-all-start.1 = ((bf16[64,16,128]{2,1,0:T(8,128)(2,1)}), bf16[64,16,128]{2,1,0:T(8,128)(2,1)S(1)}, u32[]{:S(2)}, u32[]{:S(2)}) async-start(bf16[64,16,128]{2,1,0:T(8,128)(2,1)} %bitcast.2), calls=%async_computation.1 | async-start | bytes 524288 | tf_op jit(solution)/shard_map/all_to_all | solution.py:320
  35.4 0.0 collective-permute-done.1.across_ref
  35.4 0.0 collective-permute-done.side_ref
  35.4 0.0 copy-done
  35.4 0.8 %plan.1 = (s32[64,128]{1,0:T(8,128)S(1)}, bf16[640,512]{1,0:T(8,128)(2,1)S(1)}, bf16[384,512]{1,0:T(8,128)(2,1)S(1)}) custom-call(bf16[8,48,128]{2,1,0:T(8,128)(2,1)S(1)} %all-to-all-done.got_ref, bf16[4,512,128]{2,1,0:T(8,128)(2,1)S(1)} %copy-done, bf16[4,512,128]{2,1,0:T(8,128)(2,1)S(1)} %collective-permute-done.side_ref, ...), custom_call_target="tpu_custom_call" | custom-call | flops 17179869184 | bytes 5242880 | tf_op jit(solution)/shard_map/plan/pallas_call | solution.py:241
  36.3 2.5 %collective-permute-start.2 = (bf16[384,512]{1,0:T(8,128)(2,1)S(1)}, bf16[384,512]{1,0:T(8,128)(2,1)S(1)}, u32[]{:S(2)}, u32[]{:S(2)}) collective-permute-start(bf16[384,512]{1,0:T(8,128)(2,1)S(1)} %get-tuple-element.17), channel_id=1, source_target_pairs={{0,4},{4,0},{1,5},{5,1},{2,6},{6,2},{3,7},{7,3},{8,12},{12,8},{9,1... | collective-permute-start | bytes 1179656 | tf_op jit(solution)/shard_map/ppermute | solution.py:322
  38.8 9.7 %all-to-all-done.1 = bf16[64,16,128]{2,1,0:T(8,128)(2,1)S(1)} async-done(((bf16[64,16,128]{2,1,0:T(8,128)(2,1)}), bf16[64,16,128]{2,1,0:T(8,128)(2,1)S(1)}, u32[]{:S(2)}, u32[]{:S(2)}) %all-to-all-start.1) | async-done | bytes 262176 | tf_op jit(solution)/shard_map/all_to_all | solution.py:320
  48.5 0.0 collective-permute-done.2.theirs_hbm
  48.5 2.5 %local_sums.1 = bf16[256,512]{1,0:T(8,128)(2,1)S(1)} custom-call(bf16[8,48,128]{2,1,0:T(8,128)(2,1)S(1)} %all-to-all-done.got_ref, bf16[1024,128]{1,0:T(8,128)(2,1)S(1)} %bitcast.6, s32[64,128]{1,0:T(8,128)S(1)} %get-tuple-element.15.plan_ref, bf16[640,512]{1,0:T(8,128)(2,1)S(1)} %get-tuple-element.16.ours_hbm, ...), custom_call_target="tpu_custom_call" | custom-call | flops 1073741824 | bytes 5242880 | tf_op jit(solution)/shard_map/local_sums/pallas_call | solution.py:295
  51.0 11.7 %all_to_all.25 = bf16[8,32,512]{2,1,0:T(8,128)(2,1)S(1)} all-to-all(bf16[8,32,512]{2,1,0:T(8,128)(2,1)S(1)} %bitcast.7), channel_id=1, replica_groups=mesh['y'=8,'z'=8,'c'=2,'x'=4] {'c','x'}, dimensions={0} | all-to-all | bytes 524288 | tf_op jit(solution)/shard_map/all_to_all | solution.py:324
  62.7 0.7 %convert_reduce_fusion = f32[32,512]{1,0:T(8,128)} fusion(bf16[8,32,512]{2,1,0:T(8,128)(2,1)S(1)} %all_to_all.25), kind=kLoop, calls=%fused_computation | loop fusion | flops 245760 | bytes 327680 | tf_op jit(solution)/shard_map/reduce_sum | solution.py:325
Async XLA Ops:
  4.2 17.9 %all-to-all-start = ((bf16[8,48,128]{2,1,0:T(8,128)(2,1)}), bf16[8,48,128]{2,1,0:T(8,128)(2,1)S(1)}, u32[]{:S(2)}, u32[]{:S(2)}) async-start(bf16[8,48,128]{2,1,0:T(8,128)(2,1)} %get-tuple-element.11), calls=%async_computation | async-start | bytes 196608 | tf_op jit(solution)/shard_map/all_to_all | solution.py:316
  14.3 21.0 %collective-permute-start = (bf16[4,512,128]{2,1,0:T(8,128)(2,1)}, bf16[4,512,128]{2,1,0:T(8,128)(2,1)S(1)}, u32[]{:S(2)}, u32[]{:S(2)}) collective-permute-start(bf16[4,512,128]{2,1,0:T(8,128)(2,1)} %get-tuple-element.13), channel_id=1, source_target_pairs={{0,3},{1,0},{2,1},{3,2},{4,5},{5,6},{6,7},{7,4},{8,11},{9,8},{10,9... | collective-permute-start | bytes 1572872 | tf_op jit(solution)/shard_map/ppermute | solution.py:318
  17.6 17.8 %copy-start = (bf16[4,512,128]{2,1,0:T(8,128)(2,1)S(1)}, bf16[4,512,128]{2,1,0:T(8,128)(2,1)}, u32[]{:S(2)}) copy-start(bf16[4,512,128]{2,1,0:T(8,128)(2,1)} %get-tuple-element.12.own_ref) | copy-start | bytes 1572868
  17.6 17.7 %collective-permute-start.1 = (bf16[2,512,128]{2,1,0:T(8,128)(2,1)}, bf16[2,512,128]{2,1,0:T(8,128)(2,1)S(1)}, u32[]{:S(2)}, u32[]{:S(2)}) collective-permute-start(bf16[2,512,128]{2,1,0:T(8,128)(2,1)} %get-tuple-element.14), channel_id=1, source_target_pairs={{0,2},{1,3},{2,0},{3,1},{4,6},{5,7},{6,4},{7,5},{8,10},{9,11},{10,... | collective-permute-start | bytes 786440 | tf_op jit(solution)/shard_map/ppermute | solution.py:319
  23.4 25.1 %all-to-all-start.1 = ((bf16[64,16,128]{2,1,0:T(8,128)(2,1)}), bf16[64,16,128]{2,1,0:T(8,128)(2,1)S(1)}, u32[]{:S(2)}, u32[]{:S(2)}) async-start(bf16[64,16,128]{2,1,0:T(8,128)(2,1)} %bitcast.2), calls=%async_computation.1 | async-start | bytes 524288 | tf_op jit(solution)/shard_map/all_to_all | solution.py:320
  36.3 12.2 %collective-permute-start.2 = (bf16[384,512]{1,0:T(8,128)(2,1)S(1)}, bf16[384,512]{1,0:T(8,128)(2,1)S(1)}, u32[]{:S(2)}, u32[]{:S(2)}) collective-permute-start(bf16[384,512]{1,0:T(8,128)(2,1)S(1)} %get-tuple-element.17), channel_id=1, source_target_pairs={{0,4},{4,0},{1,5},{5,1},{2,6},{6,2},{3,7},{7,3},{8,12},{12,8},{9,1... | collective-permute-start | bytes 1179656 | tf_op jit(solution)/shard_map/ppermute | solution.py:322

commit v3 on v2

--- a/solution.py
+++ b/solution.py
@@ -71,8 +71,8 @@
 
 def upward_kernel(
     count_hbm, leaves_hbm, target_hbm, source_hbm, send_hbm, inner_hbm, outer_hbm, ops_hbm,
-    parents_ref, msg_ref, own_hbm, side_hbm, across_hbm,
-    count_ref, leaves_ref, target_ref, source_ref, send_ref, inner_ref, outer_ref, own_ref, side_ref, across_ref, sems, out_sems,
+    parents_ref, msg_ref, own_ref, side_ref, across_ref,
+    count_ref, leaves_ref, target_ref, source_ref, send_ref, inner_ref, outer_ref, sems, out_sems,
 ):
     sub, core = lax.axis_index("x"), lax.axis_index("c")
     own, beside, across = [pl.multiple_of((x & 3) * LANES, LANES) for x in (sub, sub + 3 + 2 * core, sub + 2)]
@@ -86,11 +86,6 @@
         pltpu.make_async_copy(ops_hbm.at[:, :, pl.ds(beside, LANES)], side_ref, out_sems.at[0]),
         pltpu.make_async_copy(ops_hbm.at[pl.ds(2 * core, 2), :, pl.ds(across, LANES)], across_ref, out_sems.at[1]),
         pltpu.make_async_copy(ops_hbm.at[:, :, pl.ds(own, LANES)], own_ref, out_sems.at[2]),
-    ]
-    out = [
-        pltpu.make_async_copy(side_ref, side_hbm, out_sems.at[3]),
-        pltpu.make_async_copy(across_ref, across_hbm, out_sems.at[4]),
-        pltpu.make_async_copy(own_ref, own_hbm, out_sems.at[5]),
     ]
     for copy in into:
         copy.start()
@@ -113,9 +108,6 @@
     tail = jnp.concatenate([send_ref[...].astype(F32), info], axis=0).astype(BF)
     for e in range(PEERS):
         msg_ref[e, ROWS:MSG, :] = tail
-    for i in range(3):
-        into[i].wait()
-        out[i].start()
     copies[4].wait()
     sorted_leaves = dot(sort, leaves_ref[...]).astype(BF)
     copies[5].wait()
@@ -141,7 +133,7 @@
         turned = pltpu.roll(block, EIGHTH, 1)
         msg_ref[j, 0:ROWS, :] = jnp.where(lane < EIGHTH, block, turned).astype(BF)
         msg_ref[SUBS + j, 0:ROWS, :] = jnp.where(lane < EIGHTH, turned, block).astype(BF)
-    for copy in out:
+    for copy in into:
         copy.wait()
 
 
@@ -151,13 +143,13 @@
         upward_kernel,
         out_shape=(
             jax.ShapeDtypeStruct((ROWS, NODES), BF),
-            jax.ShapeDtypeStruct((PEERS, MSG, LANES), BF),
-            jax.ShapeDtypeStruct((4, NODES, LANES), BF),
-            jax.ShapeDtypeStruct((4, NODES, LANES), BF),
-            jax.ShapeDtypeStruct((2, NODES, LANES), BF),
+            pltpu.VMEM((PEERS, MSG, LANES), BF),
+            pltpu.VMEM((4, NODES, LANES), BF),
+            pltpu.VMEM((4, NODES, LANES), BF),
+            pltpu.VMEM((2, NODES, LANES), BF),
         ),
         in_specs=[anywhere] * 8,
-        out_specs=(vmem, vmem, anywhere, anywhere, anywhere),
+        out_specs=(vmem,) * 5,
         scratch_shapes=[
             pltpu.VMEM((1, 4), jnp.int32),
             pltpu.VMEM((256, NODES), BF),
@@ -166,11 +158,8 @@
             pltpu.VMEM((GHOST, SEG), jnp.int32),
             pltpu.VMEM((4 * LANES, 2 * LANES), BF),
             pltpu.VMEM((2 * NODES, NODES), BF),
-            pltpu.VMEM((4, NODES, LANES), BF),
-            pltpu.VMEM((4, NODES, LANES), BF),
-            pltpu.VMEM((2, NODES, LANES), BF),
             pltpu.SemaphoreType.DMA((7,)),
-            pltpu.SemaphoreType.DMA((6,)),
+            pltpu.SemaphoreType.DMA((3,)),
         ],
         compiler_params=pltpu.CompilerParams(vmem_limit_bytes=VMEM),
         cost_estimate=pl.CostEstimate(flops=2 * 256 * 512 * 512, bytes_accessed=5 << 20, transcendentals=0),
@@ -200,7 +189,7 @@
     vmem = pl.BlockSpec(memory_space=pltpu.VMEM)
     return pl.pallas_call(
         pick_kernel,
-        out_shape=jax.ShapeDtypeStruct((CHIPS * 16, LANES), BF),
+        out_shape=pltpu.VMEM((CHIPS * 16, LANES), BF),
         in_specs=[vmem],
         out_specs=vmem,
         compiler_params=pltpu.CompilerParams(vmem_limit_bytes=SMALL_VMEM),

time: 63.8 us -> 63 us (0.987)
  Pallas kernels: 8.22 us -> 7.54 us
    pallas_call x1, Pallas kernels: 3.53 us -> 2.83 us  [upward(): pl.pallas_call(upward_kernel, out_shape=(jax.ShapeDtypeStruct((ROWS, NODE...]
where the time goes in v3:
time: 63 us; the launch traced here: 62.6 us
  starting transfers between devices  32.2 us (51%)
  blocking collectives  11.7 us (19%)
  waiting for transfers between devices  9.75 us (15%)
  Pallas kernels  7.54 us (12%)
  between operations  0.71 us (1%)
  other arithmetic  0.67 us (1%)
    all_to_all x1, starting transfers between devices, body(): ghosts = lax.all_to_all(pick(got), ('y', 'z'), 0, 0, tiled=True)  11.9 us
    all_to_all x1, blocking collectives, body(): parts = lax.all_to_all(sums, ('c', 'x'), 0, 0, tiled=True)  11.7 us
    all_to_all x1, starting transfers between devices, body(): got = lax.all_to_all(message, ('c', 'x'), 0, 0, tiled=True)  10.2 us
    all_to_all x1, waiting for transfers between devices, body(): ghosts = lax.all_to_all(pick(got), ('y', 'z'), 0, 0, tiled=True)  9.74 us
    ppermute x1, starting transfers between devices, body(): lax.ppermute(across, 'x', [(i, (i + 2) % SUBS) for i in range(SUBS)])  4.32 us
    ppermute x1, starting transfers between devices, body(): side = lax.ppermute(side, ('c', 'x'), steps)  3.27 us
    pallas_call x1, Pallas kernels, upward(): pl.pallas_call(upward_kernel, out_shape=(jax.ShapeDtypeStruct((ROWS, NODE...  2.83 us
    pallas_call x1, Pallas kernels, local_sums(): pl.pallas_call(local_kernel, out_shape=jax.ShapeDtypeStruct((2 * SEG, NOD...  2.53 us
  transfers between devices with their start and end apart: 5, of which 1 were waited for; matrix products, arithmetic and copies ran while one was open for 0% of the time, Pallas kernels for 3%

profile of v3, /device:TPU:1, one launch (start us, length us, event | category | flops | bytes accessed | tf_op | source)
XLA Modules:
  0.0 62.6 jit_solution(11340753150262310508)
XLA Ops:
  0.6 2.8 %upward.1 = (bf16[32,512]{1,0:T(8,128)(2,1)}, bf16[8,48,128]{2,1,0:T(8,128)(2,1)}, bf16[4,512,128]{2,1,0:T(8,128)(2,1)S(1)}, bf16[4,512,128]{2,1,0:T(8,128)(2,1)S(1)}, bf16[2,512,128]{2,1,0:T(8,128)(2,1)S(1)}) custom-call(s32[1,4]{1,0:T(1,128)} %count_hbm.1, bf16[256,512]{1,0:T(8,128)(2,1)} %leaves_hbm.1, s32[1,4,128]{2,1,0:T(4,128)} %target_hbm.1, ...), custom_call_target="tpu_custom_call" | custom-call | flops 134217728 | bytes 5242880 | tf_op jit(solution)/shard_map/upward/pallas_call | solution.py:142
  3.5 10.2 %all-to-all-start = ((bf16[8,48,128]{2,1,0:T(8,128)(2,1)}), bf16[8,48,128]{2,1,0:T(8,128)(2,1)S(1)}, u32[]{:S(2)}, u32[]{:S(2)}) async-start(bf16[8,48,128]{2,1,0:T(8,128)(2,1)} %get-tuple-element.11), calls=%async_computation | async-start | bytes 196608 | tf_op jit(solution)/shard_map/all_to_all | solution.py:305
  13.6 3.3 %collective-permute-start = (bf16[4,512,128]{2,1,0:T(8,128)(2,1)S(1)}, bf16[4,512,128]{2,1,0:T(8,128)(2,1)S(1)}, u32[]{:S(2)}, u32[]{:S(2)}) collective-permute-start(bf16[4,512,128]{2,1,0:T(8,128)(2,1)S(1)} %get-tuple-element.13), channel_id=1, source_target_pairs={{0,3},{1,0},{2,1},{3,2},{4,5},{5,6},{6,7},{7,4},{8,11},{9,8},{10,9... | collective-permute-start | bytes 1572872 | tf_op jit(solution)/shard_map/ppermute | solution.py:307
  16.9 4.3 %collective-permute-start.1 = (bf16[2,512,128]{2,1,0:T(8,128)(2,1)S(1)}, bf16[2,512,128]{2,1,0:T(8,128)(2,1)S(1)}, u32[]{:S(2)}, u32[]{:S(2)}) collective-permute-start(bf16[2,512,128]{2,1,0:T(8,128)(2,1)S(1)} %get-tuple-element.14), channel_id=1, source_target_pairs={{0,2},{1,3},{2,0},{3,1},{4,6},{5,7},{6,4},{7,5},{8,10},{9,11},{10,... | collective-permute-start | bytes 786440 | tf_op jit(solution)/shard_map/ppermute | solution.py:308
  21.2 0.0 all-to-all-done.got_ref
  21.2 1.3 %pick.1 = bf16[1024,128]{1,0:T(8,128)(2,1)} custom-call(bf16[8,48,128]{2,1,0:T(8,128)(2,1)S(1)} %all-to-all-done.got_ref), custom_call_target="tpu_custom_call" | custom-call | flops 17179869184 | bytes 524288 | tf_op jit(solution)/shard_map/pick/pallas_call | solution.py:190
  22.6 11.9 %all-to-all-start.1 = ((bf16[64,16,128]{2,1,0:T(8,128)(2,1)}), bf16[64,16,128]{2,1,0:T(8,128)(2,1)S(1)}, u32[]{:S(2)}, u32[]{:S(2)}) async-start(bf16[64,16,128]{2,1,0:T(8,128)(2,1)} %bitcast.2), calls=%async_computation.1 | async-start | bytes 524288 | tf_op jit(solution)/shard_map/all_to_all | solution.py:309
  34.5 0.0 collective-permute-done.1.across_ref
  34.5 0.0 collective-permute-done.side_ref
  34.6 0.8 %plan.1 = (s32[64,128]{1,0:T(8,128)S(1)}, bf16[640,512]{1,0:T(8,128)(2,1)S(1)}, bf16[384,512]{1,0:T(8,128)(2,1)S(1)}) custom-call(bf16[8,48,128]{2,1,0:T(8,128)(2,1)S(1)} %all-to-all-done.got_ref, bf16[4,512,128]{2,1,0:T(8,128)(2,1)S(1)} %get-tuple-element.12.own_ref, bf16[4,512,128]{2,1,0:T(8,128)(2,1)S(1)} %collective-permute-done.side_ref, ...), custom_call_target="tpu_custom_call" | custom-call | flops 17179869184 | bytes 5242880 | tf_op jit(solution)/shard_map/plan/pallas_call | solution.py:230
  35.4 2.5 %collective-permute-start.2 = (bf16[384,512]{1,0:T(8,128)(2,1)S(1)}, bf16[384,512]{1,0:T(8,128)(2,1)S(1)}, u32[]{:S(2)}, u32[]{:S(2)}) collective-permute-start(bf16[384,512]{1,0:T(8,128)(2,1)S(1)} %get-tuple-element.17), channel_id=1, source_target_pairs={{0,4},{4,0},{1,5},{5,1},{2,6},{6,2},{3,7},{7,3},{8,12},{12,8},{9,1... | collective-permute-start | bytes 1179656 | tf_op jit(solution)/shard_map/ppermute | solution.py:311
  37.9 9.7 %all-to-all-done.1 = bf16[64,16,128]{2,1,0:T(8,128)(2,1)S(1)} async-done(((bf16[64,16,128]{2,1,0:T(8,128)(2,1)}), bf16[64,16,128]{2,1,0:T(8,128)(2,1)S(1)}, u32[]{:S(2)}, u32[]{:S(2)}) %all-to-all-start.1) | async-done | bytes 262176 | tf_op jit(solution)/shard_map/all_to_all | solution.py:309
  47.7 0.0 collective-permute-done.2.theirs_hbm
  47.7 2.5 %local_sums.1 = bf16[256,512]{1,0:T(8,128)(2,1)S(1)} custom-call(bf16[8,48,128]{2,1,0:T(8,128)(2,1)S(1)} %all-to-all-done.got_ref, bf16[1024,128]{1,0:T(8,128)(2,1)S(1)} %bitcast.6, s32[64,128]{1,0:T(8,128)S(1)} %get-tuple-element.15.plan_ref, bf16[640,512]{1,0:T(8,128)(2,1)S(1)} %get-tuple-element.16.ours_hbm, ...), custom_call_target="tpu_custom_call" | custom-call | flops 1073741824 | bytes 5242880 | tf_op jit(solution)/shard_map/local_sums/pallas_call | solution.py:284
  50.2 11.7 %all_to_all.25 = bf16[8,32,512]{2,1,0:T(8,128)(2,1)S(1)} all-to-all(bf16[8,32,512]{2,1,0:T(8,128)(2,1)S(1)} %bitcast.7), channel_id=1, replica_groups=mesh['y'=8,'z'=8,'c'=2,'x'=4] {'c','x'}, dimensions={0} | all-to-all | bytes 524288 | tf_op jit(solution)/shard_map/all_to_all | solution.py:313
  61.9 0.7 %convert_reduce_fusion = f32[32,512]{1,0:T(8,128)} fusion(bf16[8,32,512]{2,1,0:T(8,128)(2,1)S(1)} %all_to_all.25), kind=kLoop, calls=%fused_computation | loop fusion | flops 245760 | bytes 327680 | tf_op jit(solution)/shard_map/reduce_sum | solution.py:314
Async XLA Ops:
  3.5 17.8 %all-to-all-start = ((bf16[8,48,128]{2,1,0:T(8,128)(2,1)}), bf16[8,48,128]{2,1,0:T(8,128)(2,1)S(1)}, u32[]{:S(2)}, u32[]{:S(2)}) async-start(bf16[8,48,128]{2,1,0:T(8,128)(2,1)} %get-tuple-element.11), calls=%async_computation | async-start | bytes 196608 | tf_op jit(solution)/shard_map/all_to_all | solution.py:305
  13.6 20.9 %collective-permute-start = (bf16[4,512,128]{2,1,0:T(8,128)(2,1)S(1)}, bf16[4,512,128]{2,1,0:T(8,128)(2,1)S(1)}, u32[]{:S(2)}, u32[]{:S(2)}) collective-permute-start(bf16[4,512,128]{2,1,0:T(8,128)(2,1)S(1)} %get-tuple-element.13), channel_id=1, source_target_pairs={{0,3},{1,0},{2,1},{3,2},{4,5},{5,6},{6,7},{7,4},{8,11},{9,8},{10,9... | collective-permute-start | bytes 1572872 | tf_op jit(solution)/shard_map/ppermute | solution.py:307
  16.9 17.6 %collective-permute-start.1 = (bf16[2,512,128]{2,1,0:T(8,128)(2,1)S(1)}, bf16[2,512,128]{2,1,0:T(8,128)(2,1)S(1)}, u32[]{:S(2)}, u32[]{:S(2)}) collective-permute-start(bf16[2,512,128]{2,1,0:T(8,128)(2,1)S(1)} %get-tuple-element.14), channel_id=1, source_target_pairs={{0,2},{1,3},{2,0},{3,1},{4,6},{5,7},{6,4},{7,5},{8,10},{9,11},{10,... | collective-permute-start | bytes 786440 | tf_op jit(solution)/shard_map/ppermute | solution.py:308
  22.6 25.1 %all-to-all-start.1 = ((bf16[64,16,128]{2,1,0:T(8,128)(2,1)}), bf16[64,16,128]{2,1,0:T(8,128)(2,1)S(1)}, u32[]{:S(2)}, u32[]{:S(2)}) async-start(bf16[64,16,128]{2,1,0:T(8,128)(2,1)} %bitcast.2), calls=%async_computation.1 | async-start | bytes 524288 | tf_op jit(solution)/shard_map/all_to_all | solution.py:309
  35.4 12.3 %collective-permute-start.2 = (bf16[384,512]{1,0:T(8,128)(2,1)S(1)}, bf16[384,512]{1,0:T(8,128)(2,1)S(1)}, u32[]{:S(2)}, u32[]{:S(2)}) collective-permute-start(bf16[384,512]{1,0:T(8,128)(2,1)S(1)} %get-tuple-element.17), channel_id=1, source_target_pairs={{0,4},{4,0},{1,5},{5,1},{2,6},{6,2},{3,7},{7,3},{8,12},{12,8},{9,1... | collective-permute-start | bytes 1179656 | tf_op jit(solution)/shard_map/ppermute | solution.py:311

commit v4 on v3

--- a/solution.py
+++ b/solution.py
@@ -20,7 +20,6 @@
 PEERS = 8
 ROWS = 32
 MSG = 48
-OURS, THEIRS = 640, 384
 EIGHTH = 64
 LANES = 128
 WIDTH = 384
@@ -126,13 +125,8 @@
     total = total[0:ROWS, :] + total[ROWS:, :]
     parents = total.astype(BF)
     parents_ref[...] = parents
-    wide = parents.astype(F32)
-    lane = iota((ROWS, LANES), 1)
-    for j in range(SUBS):
-        block = wide[:, j * LANES : (j + 1) * LANES]
-        turned = pltpu.roll(block, EIGHTH, 1)
-        msg_ref[j, 0:ROWS, :] = jnp.where(lane < EIGHTH, block, turned).astype(BF)
-        msg_ref[SUBS + j, 0:ROWS, :] = jnp.where(lane < EIGHTH, turned, block).astype(BF)
+    for j in range(PEERS):
+        msg_ref[j, 0:ROWS, :] = parents[:, (j & 3) * LANES : ((j & 3) + 1) * LANES]
     for copy in into:
         copy.wait()
 
@@ -169,27 +163,21 @@
 
 def pick_kernel(got_ref, out_ref):
     parents = jnp.concatenate([got_ref[j, 0:ROWS, :] for j in range(PEERS)], axis=0)
-    lane = iota((2 * SEG, LANES), 1)
-    zero = jnp.zeros_like(parents)
-    rhs = jnp.concatenate([jnp.where(lane < EIGHTH, parents, zero), jnp.where(lane < EIGHTH, zero, parents)], axis=0)
     send = jnp.concatenate([got_ref[0, ROWS : ROWS + 8, :].astype(F32), got_ref[4, ROWS : ROWS + 8, :].astype(F32) + SEG], axis=0)
     send = send.astype(jnp.int32)
+    send = jnp.where(lax.axis_index("c") == 0, send, pltpu.roll(send, LANES - 1, 1))
     at = iota((16, 2 * SEG), 1)
     step = 16
     for first in range(0, CHIPS, step):
-        blocks = []
-        for d in range(first, first + step):
-            halves = [onehot(send[:, 2 * d + h : 2 * d + h + 1] == at) for h in range(2)]
-            blocks.append(jnp.concatenate(halves, axis=1))
-        lhs = jnp.concatenate(blocks, axis=0)
-        out_ref[first * 16 : (first + step) * 16, :] = dot(lhs, rhs).astype(BF)
+        lhs = jnp.concatenate([onehot(send[:, 2 * d : 2 * d + 1] == at) for d in range(first, first + step)], axis=0)
+        out_ref[first * 16 : (first + step) * 16, :] = dot(lhs, parents).astype(BF)
 
 
 def pick(got):
     vmem = pl.BlockSpec(memory_space=pltpu.VMEM)
     return pl.pallas_call(
         pick_kernel,
-        out_shape=pltpu.VMEM((CHIPS * 16, LANES), BF),
+        out_shape=jax.ShapeDtypeStruct((CHIPS * 16, LANES), BF),
         in_specs=[vmem],
         out_specs=vmem,
         compiler_params=pltpu.CompilerParams(vmem_limit_bytes=SMALL_VMEM),
@@ -198,105 +186,83 @@
     )(got)
 
 
-def plan_kernel(got_ref, own_ref, side_ref, across_ref, out_ref, ours_ref, theirs_ref):
+def plan_kernel(got_ref, side_ref, across_ref, out_ref, first_ref, second_ref):
     sub, core = lax.axis_index("x"), lax.axis_index("c")
-    beside = (sub + 1 + 2 * core, sub + 3 + 2 * core)
-    for q in range(2):
-        groups = []
-        for x in (sub, beside[0], beside[1], sub + 2):
-            info = got_ref[q * 4 + (x & 3), ROWS + 8 : MSG, :].astype(F32)
-            groups.append(((info[0:4, :] - 1.0) * BASE + info[4:8, :]).astype(jnp.int32))
-        first, last = groups[3][0:2, :], groups[3][2:4, :]
-        here, there = jnp.where(core == 0, first, last), jnp.where(core == 0, last, first)
-        at = q * 16
-        for source in (groups[0], groups[1], here, groups[2], there):
-            rows = source.shape[0]
-            ghost = source - SEG
-            out_ref[at : at + rows, :] = jnp.where(source < SEG, jnp.where(source < 0, -1, source + 256), ghost & 255)
-            out_ref[32 + at : 32 + at + rows, :] = jnp.where(source < SEG, 0, ghost >> 8)
-            at += rows
-    to, at = iota((EIGHTH, LANES), 0), iota((EIGHTH, LANES), 1)
-    mine, other = onehot(at == core * EIGHTH + to), onehot(at == (1 - core) * EIGHTH + to)
-    for k in range(6):
-        tile = side_ref[k] if k < 4 else across_ref[k - 4]
-        theirs_ref[k * EIGHTH : (k + 1) * EIGHTH, :] = dot_t(other, tile).astype(BF)
-        ours_ref[(4 + k) * EIGHTH : (5 + k) * EIGHTH, :] = dot_t(mine, tile).astype(BF)
-    for k in range(4):
-        ours_ref[k * EIGHTH : (k + 1) * EIGHTH, :] = dot_t(mine, own_ref[k]).astype(BF)
-
-
-def plan(got, own, side, across):
-    vmem, anywhere = pl.BlockSpec(memory_space=pltpu.VMEM), pl.BlockSpec(memory_space=pl.ANY)
+    groups = []
+    for x in (sub, sub + 1 + 2 * core, sub + 3 + 2 * core, sub + 2):
+        info = got_ref[core * 4 + (x & 3), ROWS + 8 : MSG, :].astype(F32)
+        groups.append(((info[0:4, :] - 1.0) * BASE + info[4:8, :]).astype(jnp.int32))
+    first, last = groups[3][0:2, :], groups[3][2:4, :]
+    here, there = jnp.where(core == 0, first, last), jnp.where(core == 0, last, first)
+    at = 0
+    for source in (groups[0], groups[1], here, groups[2], there):
+        rows = source.shape[0]
+        ghost = source - SEG
+        out_ref[at : at + rows, :] = jnp.where(source < SEG, jnp.where(source < 0, -1, source + 256), ghost & 255)
+        out_ref[16 + at : 16 + at + rows, :] = jnp.where(source < SEG, 0, ghost >> 8)
+        at += rows
+    first_ref[...] = side_ref[0:3]
+    second_ref[0:1] = side_ref[3:4]
+    second_ref[1:3] = across_ref[...]
+
+
+def plan(got, side, across):
+    vmem = pl.BlockSpec(memory_space=pltpu.VMEM)
     return pl.pallas_call(
         plan_kernel,
-        out_shape=(
-            jax.ShapeDtypeStruct((64, SEG), jnp.int32),
-            jax.ShapeDtypeStruct((OURS, NODES), BF),
-            jax.ShapeDtypeStruct((THEIRS, NODES), BF),
-        ),
-        in_specs=[vmem] * 4,
-        out_specs=(vmem, vmem, vmem),
+        out_shape=(jax.ShapeDtypeStruct((32, SEG), jnp.int32),) + (jax.ShapeDtypeStruct((3, NODES, LANES), BF),) * 2,
+        in_specs=[vmem] * 3,
+        out_specs=(vmem,) * 3,
         compiler_params=pltpu.CompilerParams(vmem_limit_bytes=SMALL_VMEM),
         cost_estimate=pl.CostEstimate(flops=PLAN_FLOPS, bytes_accessed=5 << 20, transcendentals=0),
         name="plan",
-    )(got, own, side, across)
-
-
-def local_kernel(got_ref, ghosts_ref, plan_ref, ours_hbm, theirs_hbm, out_ref, m_ref, rows_ref, rhs_ref, x_ref, sems):
-    copies = [
-        pltpu.make_async_copy(ours_hbm, m_ref.at[0:OURS], sems.at[0]),
-        pltpu.make_async_copy(theirs_hbm, m_ref.at[OURS:1024], sems.at[1]),
-    ]
-    for copy in copies:
-        copy.start()
+    )(got, side, across)
+
+
+def local_kernel(got_ref, ghosts_ref, plan_ref, own_ref, side_ref, across_ref, first_ref, second_ref, out_ref, rows_ref, rhs_ref, x_ref):
+    core = lax.axis_index("c")
     row = iota((WIDTH, SEG), 0)
-    for q in range(2):
-        for k in range(16):
-            at = q * 16 + k
-            rows_ref[q, :, k * SEG : (k + 1) * SEG] = onehot(plan_ref[at : at + 1, :] == row)
-    for q in range(2):
-        own = jnp.concatenate([got_ref[q * 4 + j, 0:ROWS, 0:EIGHTH] for j in range(4)], axis=0).astype(F32).T
-        rhs_ref[q, 0:EIGHTH, 256:WIDTH] = own.astype(BF)
-        rhs_ref[q, EIGHTH:256, 256:WIDTH] = jnp.zeros((256 - EIGHTH, SEG), BF)
+    for k in range(16):
+        rows_ref[:, k * SEG : (k + 1) * SEG] = onehot(plan_ref[k : k + 1, :] == row)
+    own = jnp.concatenate([got_ref[core * 4 + j, 0:ROWS, :] for j in range(4)], axis=0).astype(F32).T
+    rhs_ref[0:LANES, 256:WIDTH] = own.astype(BF)
+    rhs_ref[LANES:512, 256:WIDTH] = jnp.zeros((512 - LANES, SEG), BF)
     for b in range(4):
-        block = ghosts_ref[b * 256 : (b + 1) * 256, :].astype(F32).T.astype(BF)
-        rhs_ref[0, b * EIGHTH : (b + 1) * EIGHTH, 0:256] = block[0:EIGHTH, :]
-        rhs_ref[1, b * EIGHTH : (b + 1) * EIGHTH, 0:256] = block[EIGHTH:LANES, :]
-    for q in range(2):
-        for k in range(0, 16, 2):
-            both = dot(rhs_ref[q], rows_ref[q, :, k * SEG : (k + 2) * SEG])
-            for i in range(k, k + 2):
-                at = 32 + q * 16 + i
-                block = plan_ref[at : at + 1, :]
-                part = both[:, (i - k) * SEG : (i - k + 1) * SEG]
-                kept = jnp.where(block == 0, part[0:EIGHTH, :], 0.0)
-                for b in range(1, 4):
-                    kept = jnp.where(block == b, part[b * EIGHTH : (b + 1) * EIGHTH, :], kept)
-                x_ref[i * EIGHTH : (i + 1) * EIGHTH, q * SEG : (q + 1) * SEG] = kept.astype(BF)
-    for copy in copies:
-        copy.wait()
-    total = lax.dot_general(x_ref[...], m_ref[...], (((0,), (0,)), ((), ())), preferred_element_type=F32)
+        rhs_ref[b * LANES : (b + 1) * LANES, 0:256] = ghosts_ref[b * 256 : (b + 1) * 256, :].astype(F32).T.astype(BF)
+    total = jnp.zeros((SEG, NODES), F32)
+    for k in range(0, 16, 2):
+        both = dot(rhs_ref[...], rows_ref[:, k * SEG : (k + 2) * SEG])
+        for i in range(2):
+            block = plan_ref[16 + k + i : 17 + k + i, :]
+            part = both[:, i * SEG : (i + 1) * SEG]
+            kept = jnp.where(block == 0, part[0:LANES, :], 0.0)
+            for b in range(1, 4):
+                kept = jnp.where(block == b, part[b * LANES : (b + 1) * LANES, :], kept)
+            x_ref[(k + i) * LANES : (k + i + 1) * LANES, :] = kept.astype(BF)
+    held = ((own_ref, 4), (side_ref, 4), (across_ref, 2), (first_ref, 3), (second_ref, 3))
+    refs = [ref.at[k] for ref, count in held for k in range(count)]
+    for k in range(0, 16, 2):
+        pair = jnp.concatenate([refs[k][...], refs[k + 1][...]], axis=1)
+        total = total + lax.dot_general(x_ref[k * LANES : (k + 2) * LANES, :], pair, (((0,), (1,)), ((), ())), preferred_element_type=F32)
     out_ref[...] = total.astype(BF)
 
 
-def local_sums(got, ghosts, columns, ours, theirs):
-    vmem, anywhere = pl.BlockSpec(memory_space=pltpu.VMEM), pl.BlockSpec(memory_space=pl.ANY)
+def local_sums(got, ghosts, columns, *ops):
+    vmem = pl.BlockSpec(memory_space=pltpu.VMEM)
     return pl.pallas_call(
         local_kernel,
-        out_shape=jax.ShapeDtypeStruct((2 * SEG, NODES), BF),
-        in_specs=[vmem] * 3 + [anywhere] * 2,
+        out_shape=jax.ShapeDtypeStruct((SEG, NODES), BF),
+        in_specs=[vmem] * 8,
         out_specs=vmem,
         scratch_shapes=[
-            pltpu.VMEM((1024, NODES), BF),
-            pltpu.VMEM((2, WIDTH, 16 * SEG), BF),
-            pltpu.VMEM((2, 256, WIDTH), BF),
-            pltpu.VMEM((1024, 2 * SEG), BF),
-            pltpu.SemaphoreType.DMA((2,)),
+            pltpu.VMEM((WIDTH, 16 * SEG), BF),
+            pltpu.VMEM((512, WIDTH), BF),
+            pltpu.VMEM((16 * LANES, SEG), BF),
         ],
         compiler_params=pltpu.CompilerParams(vmem_limit_bytes=SMALL_VMEM),
         cost_estimate=pl.CostEstimate(flops=2 * 4096 * 512 * 256, bytes_accessed=5 << 20, transcendentals=0),
         name="local_sums",
-    )(got, ghosts, columns, ours, theirs)
+    )(got, ghosts, columns, *ops)
 
 
 def body(factors, leaves, m2l_ops, send_index, pair_target, pair_source, pair_count):
@@ -307,11 +273,12 @@
     side = lax.ppermute(side, ("c", "x"), steps)
     across = lax.ppermute(across, "x", [(i, (i + 2) % SUBS) for i in range(SUBS)])
     ghosts = lax.all_to_all(pick(got), ("y", "z"), 0, 0, tiled=True)
-    columns, ours, theirs = plan(got, own, side, across)
-    theirs = lax.ppermute(theirs, "c", [(0, 1), (1, 0)])
-    sums = local_sums(got, ghosts, columns, ours, theirs)
-    parts = lax.all_to_all(sums, ("c", "x"), 0, 0, tiled=True)
-    local = jnp.sum(parts.reshape(PEERS, ROWS, NODES).astype(F32), axis=0)
+    columns, first, second = plan(got, side, across)
+    first = lax.ppermute(first, "c", [(0, 1), (1, 0)])
+    second = lax.ppermute(second, "c", [(0, 1), (1, 0)])
+    sums = local_sums(got, ghosts, columns, own, side, across, first, second)
+    parts = lax.all_to_all(sums, "x", 0, 0, tiled=True)
+    local = jnp.sum(parts.reshape(SUBS, ROWS, NODES).astype(F32), axis=0)
     return (parents, local)
 
 

time: 63 us -> 59.3 us (0.941)
  the two profiles are of different devices: /device:TPU:1 before, /device:TPU:2 now
where the time goes in v4:
time: 59.3 us; the launch traced here: 58.9 us
  starting transfers between devices  32.5 us (55%)
  waiting for transfers between devices  9.86 us (17%)
  blocking collectives  9.06 us (15%)
  Pallas kernels  6.13 us (10%)
  between operations  0.72 us (1%)
  other arithmetic  0.65 us (1%)
    all_to_all x1, starting transfers between devices, body(): ghosts = lax.all_to_all(pick(got), ('y', 'z'), 0, 0, tiled=True)  12.2 us
    all_to_all x1, waiting for transfers between devices, body(): ghosts = lax.all_to_all(pick(got), ('y', 'z'), 0, 0, tiled=True)  9.85 us
    all_to_all x1, starting transfers between devices, body(): got = lax.all_to_all(message, ('c', 'x'), 0, 0, tiled=True)  9.18 us
    all_to_all x1, blocking collectives, body(): parts = lax.all_to_all(sums, 'x', 0, 0, tiled=True)  9.06 us
    ppermute x1, starting transfers between devices, body(): lax.ppermute(across, 'x', [(i, (i + 2) % SUBS) for i in range(SUBS)])  4.72 us
    pallas_call x1, Pallas kernels, upward(): pl.pallas_call(upward_kernel, out_shape=(jax.ShapeDtypeStruct((ROWS, NODE...  2.75 us
    ppermute x1, starting transfers between devices, body(): second = lax.ppermute(second, 'c', [(0, 1), (1, 0)])  2.41 us
    pallas_call x1, Pallas kernels, local_sums(): pl.pallas_call(local_kernel, out_shape=jax.ShapeDtypeStruct((SEG, NODES),...  2.13 us
  transfers between devices with their start and end apart: 6, of which 1 were waited for; matrix products, arithmetic and copies ran while one was open for 0% of the time, Pallas kernels for 2%

profile of v4, /device:TPU:2, one launch (start us, length us, event | category | flops | bytes accessed | tf_op | source)
XLA Modules:
  0.0 58.9 jit_solution(10743679030400904319)
XLA Ops:
  0.6 2.7 %upward.1 = (bf16[32,512]{1,0:T(8,128)(2,1)}, bf16[8,48,128]{2,1,0:T(8,128)(2,1)}, bf16[4,512,128]{2,1,0:T(8,128)(2,1)S(1)}, bf16[4,512,128]{2,1,0:T(8,128)(2,1)S(1)}, bf16[2,512,128]{2,1,0:T(8,128)(2,1)S(1)}) custom-call(s32[1,4]{1,0:T(1,128)} %count_hbm.1, bf16[256,512]{1,0:T(8,128)(2,1)} %leaves_hbm.1, s32[1,4,128]{2,1,0:T(4,128)} %target_hbm.1, ...), custom_call_target="tpu_custom_call" | custom-call | flops 134217728 | bytes 5242880 | tf_op jit(solution)/shard_map/upward/pallas_call | solution.py:136
  3.4 9.2 %all-to-all-start = ((bf16[8,48,128]{2,1,0:T(8,128)(2,1)}), bf16[8,48,128]{2,1,0:T(8,128)(2,1)S(1)}, u32[]{:S(2)}, u32[]{:S(2)}) async-start(bf16[8,48,128]{2,1,0:T(8,128)(2,1)} %get-tuple-element.11), calls=%async_computation | async-start | bytes 196608 | tf_op jit(solution)/shard_map/all_to_all | solution.py:271
  12.6 2.0 %collective-permute-start = (bf16[4,512,128]{2,1,0:T(8,128)(2,1)S(1)}, bf16[4,512,128]{2,1,0:T(8,128)(2,1)S(1)}, u32[]{:S(2)}, u32[]{:S(2)}) collective-permute-start(bf16[4,512,128]{2,1,0:T(8,128)(2,1)S(1)} %get-tuple-element.12), channel_id=1, source_target_pairs={{0,3},{1,0},{2,1},{3,2},{4,5},{5,6},{6,7},{7,4},{8,11},{9,8},{10,9... | collective-permute-start | bytes 1572872 | tf_op jit(solution)/shard_map/ppermute | solution.py:273
  14.6 4.7 %collective-permute-start.1 = (bf16[2,512,128]{2,1,0:T(8,128)(2,1)S(1)}, bf16[2,512,128]{2,1,0:T(8,128)(2,1)S(1)}, u32[]{:S(2)}, u32[]{:S(2)}) collective-permute-start(bf16[2,512,128]{2,1,0:T(8,128)(2,1)S(1)} %get-tuple-element.13), channel_id=1, source_target_pairs={{0,2},{1,3},{2,0},{3,1},{4,6},{5,7},{6,4},{7,5},{8,10},{9,11},{10,... | collective-permute-start | bytes 786440 | tf_op jit(solution)/shard_map/ppermute | solution.py:274
  19.3 0.0 all-to-all-done.got_ref
  19.3 1.2 %pick.1 = bf16[1024,128]{1,0:T(8,128)(2,1)} custom-call(bf16[8,48,128]{2,1,0:T(8,128)(2,1)S(1)} %all-to-all-done.got_ref), custom_call_target="tpu_custom_call" | custom-call | flops 17179869184 | bytes 524288 | tf_op jit(solution)/shard_map/pick/pallas_call | solution.py:178
  20.5 12.2 %all-to-all-start.1 = ((bf16[64,16,128]{2,1,0:T(8,128)(2,1)}), bf16[64,16,128]{2,1,0:T(8,128)(2,1)S(1)}, u32[]{:S(2)}, u32[]{:S(2)}) async-start(bf16[64,16,128]{2,1,0:T(8,128)(2,1)} %bitcast.2), calls=%async_computation.1 | async-start | bytes 524288 | tf_op jit(solution)/shard_map/all_to_all | solution.py:275
  32.8 0.0 collective-permute-done.1.across_ref
  32.8 0.0 collective-permute-done.side_ref
  32.8 0.1 plan.1
  32.9 1.9 %collective-permute-start.2 = (bf16[3,512,128]{2,1,0:T(8,128)(2,1)S(1)}, bf16[3,512,128]{2,1,0:T(8,128)(2,1)S(1)}, u32[]{:S(2)}, u32[]{:S(2)}) collective-permute-start(bf16[3,512,128]{2,1,0:T(8,128)(2,1)S(1)} %get-tuple-element.16), channel_id=1, source_target_pairs={{0,4},{4,0},{1,5},{5,1},{2,6},{6,2},{3,7},{7,3},{8,12},{12,8},{9,1... | collective-permute-start | bytes 1179656 | tf_op jit(solution)/shard_map/ppermute | solution.py:277
  34.8 2.4 %collective-permute-start.3 = (bf16[3,512,128]{2,1,0:T(8,128)(2,1)S(1)}, bf16[3,512,128]{2,1,0:T(8,128)(2,1)S(1)}, u32[]{:S(2)}, u32[]{:S(2)}) collective-permute-start(bf16[3,512,128]{2,1,0:T(8,128)(2,1)S(1)} %get-tuple-element.17), channel_id=1, source_target_pairs={{0,4},{4,0},{1,5},{5,1},{2,6},{6,2},{3,7},{7,3},{8,12},{12,8},{9,1... | collective-permute-start | bytes 1179656 | tf_op jit(solution)/shard_map/ppermute | solution.py:278
  37.2 9.8 %all-to-all-done.1 = bf16[64,16,128]{2,1,0:T(8,128)(2,1)S(1)} async-done(((bf16[64,16,128]{2,1,0:T(8,128)(2,1)}), bf16[64,16,128]{2,1,0:T(8,128)(2,1)S(1)}, u32[]{:S(2)}, u32[]{:S(2)}) %all-to-all-start.1) | async-done | bytes 262176 | tf_op jit(solution)/shard_map/all_to_all | solution.py:275
  47.1 0.0 collective-permute-done.2.first_ref
  47.1 0.0 collective-permute-done.3.second_ref
  47.1 2.1 %local_sums.1 = bf16[128,512]{1,0:T(8,128)(2,1)S(1)} custom-call(bf16[8,48,128]{2,1,0:T(8,128)(2,1)S(1)} %all-to-all-done.got_ref, bf16[1024,128]{1,0:T(8,128)(2,1)S(1)} %bitcast.6, s32[32,128]{1,0:T(8,128)S(1)} %get-tuple-element.14.plan_ref, bf16[4,512,128]{2,1,0:T(8,128)(2,1)S(1)} %get-tuple-element.15.own_ref, ...), custom_call_target="tpu_custom_call" | custom-call | flops 1073741824 | bytes 5242880 | tf_op jit(solution)/shard_map/local_sums/pallas_call | solution.py:252
  49.2 9.1 %all_to_all.25 = bf16[4,32,512]{2,1,0:T(8,128)(2,1)S(1)} all-to-all(bf16[4,32,512]{2,1,0:T(8,128)(2,1)S(1)} %bitcast.7), channel_id=1, replica_groups=mesh['y'=8,'z'=8,'c'=2,'x'=4] {'x'}, dimensions={0} | all-to-all | bytes 262144 | tf_op jit(solution)/shard_map/all_to_all | solution.py:280
  58.3 0.6 %convert_reduce_fusion = f32[32,512]{1,0:T(8,128)} fusion(bf16[4,32,512]{2,1,0:T(8,128)(2,1)S(1)} %all_to_all.25), kind=kLoop, calls=%fused_computation | loop fusion | flops 114688 | bytes 196608 | tf_op jit(solution)/shard_map/reduce_sum | solution.py:281
Async XLA Ops:
  3.4 15.9 %all-to-all-start = ((bf16[8,48,128]{2,1,0:T(8,128)(2,1)}), bf16[8,48,128]{2,1,0:T(8,128)(2,1)S(1)}, u32[]{:S(2)}, u32[]{:S(2)}) async-start(bf16[8,48,128]{2,1,0:T(8,128)(2,1)} %get-tuple-element.11), calls=%async_computation | async-start | bytes 196608 | tf_op jit(solution)/shard_map/all_to_all | solution.py:271
  12.6 20.2 %collective-permute-start = (bf16[4,512,128]{2,1,0:T(8,128)(2,1)S(1)}, bf16[4,512,128]{2,1,0:T(8,128)(2,1)S(1)}, u32[]{:S(2)}, u32[]{:S(2)}) collective-permute-start(bf16[4,512,128]{2,1,0:T(8,128)(2,1)S(1)} %get-tuple-element.12), channel_id=1, source_target_pairs={{0,3},{1,0},{2,1},{3,2},{4,5},{5,6},{6,7},{7,4},{8,11},{9,8},{10,9... | collective-permute-start | bytes 1572872 | tf_op jit(solution)/shard_map/ppermute | solution.py:273
  14.6 18.2 %collective-permute-start.1 = (bf16[2,512,128]{2,1,0:T(8,128)(2,1)S(1)}, bf16[2,512,128]{2,1,0:T(8,128)(2,1)S(1)}, u32[]{:S(2)}, u32[]{:S(2)}) collective-permute-start(bf16[2,512,128]{2,1,0:T(8,128)(2,1)S(1)} %get-tuple-element.13), channel_id=1, source_target_pairs={{0,2},{1,3},{2,0},{3,1},{4,6},{5,7},{6,4},{7,5},{8,10},{9,11},{10,... | collective-permute-start | bytes 786440 | tf_op jit(solution)/shard_map/ppermute | solution.py:274
  20.5 26.5 %all-to-all-start.1 = ((bf16[64,16,128]{2,1,0:T(8,128)(2,1)}), bf16[64,16,128]{2,1,0:T(8,128)(2,1)S(1)}, u32[]{:S(2)}, u32[]{:S(2)}) async-start(bf16[64,16,128]{2,1,0:T(8,128)(2,1)} %bitcast.2), calls=%async_computation.1 | async-start | bytes 524288 | tf_op jit(solution)/shard_map/all_to_all | solution.py:275
  32.9 14.2 %collective-permute-start.2 = (bf16[3,512,128]{2,1,0:T(8,128)(2,1)S(1)}, bf16[3,512,128]{2,1,0:T(8,128)(2,1)S(1)}, u32[]{:S(2)}, u32[]{:S(2)}) collective-permute-start(bf16[3,512,128]{2,1,0:T(8,128)(2,1)S(1)} %get-tuple-element.16), channel_id=1, source_target_pairs={{0,4},{4,0},{1,5},{5,1},{2,6},{6,2},{3,7},{7,3},{8,12},{12,8},{9,1... | collective-permute-start | bytes 1179656 | tf_op jit(solution)/shard_map/ppermute | solution.py:277
  34.8 12.3 %collective-permute-start.3 = (bf16[3,512,128]{2,1,0:T(8,128)(2,1)S(1)}, bf16[3,512,128]{2,1,0:T(8,128)(2,1)S(1)}, u32[]{:S(2)}, u32[]{:S(2)}) collective-permute-start(bf16[3,512,128]{2,1,0:T(8,128)(2,1)S(1)} %get-tuple-element.17), channel_id=1, source_target_pairs={{0,4},{4,0},{1,5},{5,1},{2,6},{6,2},{3,7},{7,3},{8,12},{12,8},{9,1... | collective-permute-start | bytes 1179656 | tf_op jit(solution)/shard_map/ppermute | solution.py:278

commit v5 on v4

--- a/solution.py
+++ b/solution.py
@@ -22,7 +22,7 @@
 MSG = 48
 EIGHTH = 64
 LANES = 128
-WIDTH = 384
+WIDTH = 640
 PLAN_FLOPS = 1 << 34
 VMEM = 60 << 20
 SMALL_VMEM = 16 << 20
@@ -198,8 +198,8 @@
     for source in (groups[0], groups[1], here, groups[2], there):
         rows = source.shape[0]
         ghost = source - SEG
-        out_ref[at : at + rows, :] = jnp.where(source < SEG, jnp.where(source < 0, -1, source + 256), ghost & 255)
-        out_ref[16 + at : 16 + at + rows, :] = jnp.where(source < SEG, 0, ghost >> 8)
+        out_ref[at : at + rows, :] = jnp.where(source < SEG, jnp.where(source < 0, -1, source + 512), ghost & 511)
+        out_ref[16 + at : 16 + at + rows, :] = jnp.where(source < SEG, 0, ghost >> 9)
         at += rows
     first_ref[...] = side_ref[0:3]
     second_ref[0:1] = side_ref[3:4]
@@ -225,10 +225,10 @@
     for k in range(16):
         rows_ref[:, k * SEG : (k + 1) * SEG] = onehot(plan_ref[k : k + 1, :] == row)
     own = jnp.concatenate([got_ref[core * 4 + j, 0:ROWS, :] for j in range(4)], axis=0).astype(F32).T
-    rhs_ref[0:LANES, 256:WIDTH] = own.astype(BF)
-    rhs_ref[LANES:512, 256:WIDTH] = jnp.zeros((512 - LANES, SEG), BF)
-    for b in range(4):
-        rhs_ref[b * LANES : (b + 1) * LANES, 0:256] = ghosts_ref[b * 256 : (b + 1) * 256, :].astype(F32).T.astype(BF)
+    rhs_ref[0:LANES, 512:WIDTH] = own.astype(BF)
+    rhs_ref[LANES:256, 512:WIDTH] = jnp.zeros((LANES, SEG), BF)
+    for b in range(2):
+        rhs_ref[b * LANES : (b + 1) * LANES, 0:512] = ghosts_ref[b * 512 : (b + 1) * 512, :].astype(F32).T.astype(BF)
     total = jnp.zeros((SEG, NODES), F32)
     for k in range(0, 16, 2):
         both = dot(rhs_ref[...], rows_ref[:, k * SEG : (k + 2) * SEG])
@@ -236,14 +236,13 @@
             block = plan_ref[16 + k + i : 17 + k + i, :]
             part = both[:, i * SEG : (i + 1) * SEG]
             kept = jnp.where(block == 0, part[0:LANES, :], 0.0)
-            for b in range(1, 4):
+            for b in range(1, 2):
                 kept = jnp.where(block == b, part[b * LANES : (b + 1) * LANES, :], kept)
             x_ref[(k + i) * LANES : (k + i + 1) * LANES, :] = kept.astype(BF)
     held = ((own_ref, 4), (side_ref, 4), (across_ref, 2), (first_ref, 3), (second_ref, 3))
     refs = [ref.at[k] for ref, count in held for k in range(count)]
-    for k in range(0, 16, 2):
-        pair = jnp.concatenate([refs[k][...], refs[k + 1][...]], axis=1)
-        total = total + lax.dot_general(x_ref[k * LANES : (k + 2) * LANES, :], pair, (((0,), (1,)), ((), ())), preferred_element_type=F32)
+    for k in range(16):
+        total = total + lax.dot_general(x_ref[k * LANES : (k + 1) * LANES, :], refs[k][...], (((0,), (1,)), ((), ())), preferred_element_type=F32)
     out_ref[...] = total.astype(BF)
 
 
@@ -256,7 +255,7 @@
         out_specs=vmem,
         scratch_shapes=[
             pltpu.VMEM((WIDTH, 16 * SEG), BF),
-            pltpu.VMEM((512, WIDTH), BF),
+            pltpu.VMEM((256, WIDTH), BF),
             pltpu.VMEM((16 * LANES, SEG), BF),
         ],
         compiler_params=pltpu.CompilerParams(vmem_limit_bytes=SMALL_VMEM),

time: 59.3 us -> 59.1 us (level)
  no operation moved by 1% of the time
where the time goes in v5:
time: 59.1 us; the launch traced here: 58.7 us
  starting transfers between devices  32.5 us (55%)
  waiting for transfers between devices  9.86 us (17%)
  blocking collectives  9.06 us (15%)
  Pallas kernels  5.89 us (10%)
  between operations  0.72 us (1%)
  other arithmetic  0.65 us (1%)
    all_to_all x1, starting transfers between devices, body(): ghosts = lax.all_to_all(pick(got), ('y', 'z'), 0, 0, tiled=True)  12.2 us
    all_to_all x1, waiting for transfers between devices, body(): ghosts = lax.all_to_all(pick(got), ('y', 'z'), 0, 0, tiled=True)  9.85 us
    all_to_all x1, starting transfers between devices, body(): got = lax.all_to_all(message, ('c', 'x'), 0, 0, tiled=True)  9.18 us
    all_to_all x1, blocking collectives, body(): parts = lax.all_to_all(sums, 'x', 0, 0, tiled=True)  9.06 us
    ppermute x1, starting transfers between devices, body(): lax.ppermute(across, 'x', [(i, (i + 2) % SUBS) for i in range(SUBS)])  4.72 us
    pallas_call x1, Pallas kernels, upward(): pl.pallas_call(upward_kernel, out_shape=(jax.ShapeDtypeStruct((ROWS, NODE...  2.75 us
    ppermute x1, starting transfers between devices, body(): second = lax.ppermute(second, 'c', [(0, 1), (1, 0)])  2.41 us
    ppermute x1, starting transfers between devices, body(): side = lax.ppermute(side, ('c', 'x'), steps)  2.01 us
  transfers between devices with their start and end apart: 6, of which 1 were waited for; matrix products, arithmetic and copies ran while one was open for 0% of the time, Pallas kernels for 2%

profile of v5, /device:TPU:2, one launch (start us, length us, event | category | flops | bytes accessed | tf_op | source)
XLA Modules:
  0.0 58.7 jit_solution(14150791559372927244)
XLA Ops:
  0.6 2.7 %upward.1 = (bf16[32,512]{1,0:T(8,128)(2,1)}, bf16[8,48,128]{2,1,0:T(8,128)(2,1)}, bf16[4,512,128]{2,1,0:T(8,128)(2,1)S(1)}, bf16[4,512,128]{2,1,0:T(8,128)(2,1)S(1)}, bf16[2,512,128]{2,1,0:T(8,128)(2,1)S(1)}) custom-call(s32[1,4]{1,0:T(1,128)} %count_hbm.1, bf16[256,512]{1,0:T(8,128)(2,1)} %leaves_hbm.1, s32[1,4,128]{2,1,0:T(4,128)} %target_hbm.1, ...), custom_call_target="tpu_custom_call" | custom-call | flops 134217728 | bytes 5242880 | tf_op jit(solution)/shard_map/upward/pallas_call | solution.py:136
  3.4 9.2 %all-to-all-start = ((bf16[8,48,128]{2,1,0:T(8,128)(2,1)}), bf16[8,48,128]{2,1,0:T(8,128)(2,1)S(1)}, u32[]{:S(2)}, u32[]{:S(2)}) async-start(bf16[8,48,128]{2,1,0:T(8,128)(2,1)} %get-tuple-element.11), calls=%async_computation | async-start | bytes 196608 | tf_op jit(solution)/shard_map/all_to_all | solution.py:270
  12.6 2.0 %collective-permute-start = (bf16[4,512,128]{2,1,0:T(8,128)(2,1)S(1)}, bf16[4,512,128]{2,1,0:T(8,128)(2,1)S(1)}, u32[]{:S(2)}, u32[]{:S(2)}) collective-permute-start(bf16[4,512,128]{2,1,0:T(8,128)(2,1)S(1)} %get-tuple-element.12), channel_id=1, source_target_pairs={{0,3},{1,0},{2,1},{3,2},{4,5},{5,6},{6,7},{7,4},{8,11},{9,8},{10,9... | collective-permute-start | bytes 1572872 | tf_op jit(solution)/shard_map/ppermute | solution.py:272
  14.6 4.7 %collective-permute-start.1 = (bf16[2,512,128]{2,1,0:T(8,128)(2,1)S(1)}, bf16[2,512,128]{2,1,0:T(8,128)(2,1)S(1)}, u32[]{:S(2)}, u32[]{:S(2)}) collective-permute-start(bf16[2,512,128]{2,1,0:T(8,128)(2,1)S(1)} %get-tuple-element.13), channel_id=1, source_target_pairs={{0,2},{1,3},{2,0},{3,1},{4,6},{5,7},{6,4},{7,5},{8,10},{9,11},{10,... | collective-permute-start | bytes 786440 | tf_op jit(solution)/shard_map/ppermute | solution.py:273
  19.3 0.0 all-to-all-done.got_ref
  19.3 1.2 %pick.1 = bf16[1024,128]{1,0:T(8,128)(2,1)} custom-call(bf16[8,48,128]{2,1,0:T(8,128)(2,1)S(1)} %all-to-all-done.got_ref), custom_call_target="tpu_custom_call" | custom-call | flops 17179869184 | bytes 524288 | tf_op jit(solution)/shard_map/pick/pallas_call | solution.py:178
  20.5 12.2 %all-to-all-start.1 = ((bf16[64,16,128]{2,1,0:T(8,128)(2,1)}), bf16[64,16,128]{2,1,0:T(8,128)(2,1)S(1)}, u32[]{:S(2)}, u32[]{:S(2)}) async-start(bf16[64,16,128]{2,1,0:T(8,128)(2,1)} %bitcast.2), calls=%async_computation.1 | async-start | bytes 524288 | tf_op jit(solution)/shard_map/all_to_all | solution.py:274
  32.8 0.0 collective-permute-done.1.across_ref
  32.8 0.0 collective-permute-done.side_ref
  32.8 0.1 plan.1
  32.9 1.9 %collective-permute-start.2 = (bf16[3,512,128]{2,1,0:T(8,128)(2,1)S(1)}, bf16[3,512,128]{2,1,0:T(8,128)(2,1)S(1)}, u32[]{:S(2)}, u32[]{:S(2)}) collective-permute-start(bf16[3,512,128]{2,1,0:T(8,128)(2,1)S(1)} %get-tuple-element.16), channel_id=1, source_target_pairs={{0,4},{4,0},{1,5},{5,1},{2,6},{6,2},{3,7},{7,3},{8,12},{12,8},{9,1... | collective-permute-start | bytes 1179656 | tf_op jit(solution)/shard_map/ppermute | solution.py:276
  34.8 2.4 %collective-permute-start.3 = (bf16[3,512,128]{2,1,0:T(8,128)(2,1)S(1)}, bf16[3,512,128]{2,1,0:T(8,128)(2,1)S(1)}, u32[]{:S(2)}, u32[]{:S(2)}) collective-permute-start(bf16[3,512,128]{2,1,0:T(8,128)(2,1)S(1)} %get-tuple-element.17), channel_id=1, source_target_pairs={{0,4},{4,0},{1,5},{5,1},{2,6},{6,2},{3,7},{7,3},{8,12},{12,8},{9,1... | collective-permute-start | bytes 1179656 | tf_op jit(solution)/shard_map/ppermute | solution.py:277
  37.2 9.8 %all-to-all-done.1 = bf16[64,16,128]{2,1,0:T(8,128)(2,1)S(1)} async-done(((bf16[64,16,128]{2,1,0:T(8,128)(2,1)}), bf16[64,16,128]{2,1,0:T(8,128)(2,1)S(1)}, u32[]{:S(2)}, u32[]{:S(2)}) %all-to-all-start.1) | async-done | bytes 262176 | tf_op jit(solution)/shard_map/all_to_all | solution.py:274
  47.1 0.0 collective-permute-done.2.first_ref
  47.1 0.0 collective-permute-done.3.second_ref
  47.1 1.9 %local_sums.1 = bf16[128,512]{1,0:T(8,128)(2,1)S(1)} custom-call(bf16[8,48,128]{2,1,0:T(8,128)(2,1)S(1)} %all-to-all-done.got_ref, bf16[1024,128]{1,0:T(8,128)(2,1)S(1)} %bitcast.6, s32[32,128]{1,0:T(8,128)S(1)} %get-tuple-element.14.plan_ref, bf16[4,512,128]{2,1,0:T(8,128)(2,1)S(1)} %get-tuple-element.15.own_ref, ...), custom_call_target="tpu_custom_call" | custom-call | flops 1073741824 | bytes 5242880 | tf_op jit(solution)/shard_map/local_sums/pallas_call | solution.py:251
  49.0 9.1 %all_to_all.25 = bf16[4,32,512]{2,1,0:T(8,128)(2,1)S(1)} all-to-all(bf16[4,32,512]{2,1,0:T(8,128)(2,1)S(1)} %bitcast.7), channel_id=1, replica_groups=mesh['y'=8,'z'=8,'c'=2,'x'=4] {'x'}, dimensions={0} | all-to-all | bytes 262144 | tf_op jit(solution)/shard_map/all_to_all | solution.py:279
  58.0 0.6 %convert_reduce_fusion = f32[32,512]{1,0:T(8,128)} fusion(bf16[4,32,512]{2,1,0:T(8,128)(2,1)S(1)} %all_to_all.25), kind=kLoop, calls=%fused_computation | loop fusion | flops 114688 | bytes 196608 | tf_op jit(solution)/shard_map/reduce_sum | solution.py:280
Async XLA Ops:
  3.4 15.9 %all-to-all-start = ((bf16[8,48,128]{2,1,0:T(8,128)(2,1)}), bf16[8,48,128]{2,1,0:T(8,128)(2,1)S(1)}, u32[]{:S(2)}, u32[]{:S(2)}) async-start(bf16[8,48,128]{2,1,0:T(8,128)(2,1)} %get-tuple-element.11), calls=%async_computation | async-start | bytes 196608 | tf_op jit(solution)/shard_map/all_to_all | solution.py:270
  12.6 20.2 %collective-permute-start = (bf16[4,512,128]{2,1,0:T(8,128)(2,1)S(1)}, bf16[4,512,128]{2,1,0:T(8,128)(2,1)S(1)}, u32[]{:S(2)}, u32[]{:S(2)}) collective-permute-start(bf16[4,512,128]{2,1,0:T(8,128)(2,1)S(1)} %get-tuple-element.12), channel_id=1, source_target_pairs={{0,3},{1,0},{2,1},{3,2},{4,5},{5,6},{6,7},{7,4},{8,11},{9,8},{10,9... | collective-permute-start | bytes 1572872 | tf_op jit(solution)/shard_map/ppermute | solution.py:272
  14.6 18.2 %collective-permute-start.1 = (bf16[2,512,128]{2,1,0:T(8,128)(2,1)S(1)}, bf16[2,512,128]{2,1,0:T(8,128)(2,1)S(1)}, u32[]{:S(2)}, u32[]{:S(2)}) collective-permute-start(bf16[2,512,128]{2,1,0:T(8,128)(2,1)S(1)} %get-tuple-element.13), channel_id=1, source_target_pairs={{0,2},{1,3},{2,0},{3,1},{4,6},{5,7},{6,4},{7,5},{8,10},{9,11},{10,... | collective-permute-start | bytes 786440 | tf_op jit(solution)/shard_map/ppermute | solution.py:273
  20.5 26.5 %all-to-all-start.1 = ((bf16[64,16,128]{2,1,0:T(8,128)(2,1)}), bf16[64,16,128]{2,1,0:T(8,128)(2,1)S(1)}, u32[]{:S(2)}, u32[]{:S(2)}) async-start(bf16[64,16,128]{2,1,0:T(8,128)(2,1)} %bitcast.2), calls=%async_computation.1 | async-start | bytes 524288 | tf_op jit(solution)/shard_map/all_to_all | solution.py:274
  32.9 14.2 %collective-permute-start.2 = (bf16[3,512,128]{2,1,0:T(8,128)(2,1)S(1)}, bf16[3,512,128]{2,1,0:T(8,128)(2,1)S(1)}, u32[]{:S(2)}, u32[]{:S(2)}) collective-permute-start(bf16[3,512,128]{2,1,0:T(8,128)(2,1)S(1)} %get-tuple-element.16), channel_id=1, source_target_pairs={{0,4},{4,0},{1,5},{5,1},{2,6},{6,2},{3,7},{7,3},{8,12},{12,8},{9,1... | collective-permute-start | bytes 1179656 | tf_op jit(solution)/shard_map/ppermute | solution.py:276
  34.8 12.3 %collective-permute-start.3 = (bf16[3,512,128]{2,1,0:T(8,128)(2,1)S(1)}, bf16[3,512,128]{2,1,0:T(8,128)(2,1)S(1)}, u32[]{:S(2)}, u32[]{:S(2)}) collective-permute-start(bf16[3,512,128]{2,1,0:T(8,128)(2,1)S(1)} %get-tuple-element.17), channel_id=1, source_target_pairs={{0,4},{4,0},{1,5},{5,1},{2,6},{6,2},{3,7},{7,3},{8,12},{12,8},{9,1... | collective-permute-start | bytes 1179656 | tf_op jit(solution)/shard_map/ppermute | solution.py:277

commit v6 on v5

--- a/solution.py
+++ b/solution.py
@@ -221,9 +221,11 @@
 
 def local_kernel(got_ref, ghosts_ref, plan_ref, own_ref, side_ref, across_ref, first_ref, second_ref, out_ref, rows_ref, rhs_ref, x_ref):
     core = lax.axis_index("c")
-    row = iota((WIDTH, SEG), 0)
+    row = iota((WIDTH, SEG), 0).astype(jnp.int16)
+    place = plan_ref[0:16, :].astype(jnp.int16)
+    one, zero = jnp.ones((WIDTH, SEG), BF), jnp.zeros((WIDTH, SEG), BF)
     for k in range(16):
-        rows_ref[:, k * SEG : (k + 1) * SEG] = onehot(plan_ref[k : k + 1, :] == row)
+        rows_ref[:, k * SEG : (k + 1) * SEG] = jnp.where(place[k : k + 1, :] == row, one, zero)
     own = jnp.concatenate([got_ref[core * 4 + j, 0:ROWS, :] for j in range(4)], axis=0).astype(F32).T
     rhs_ref[0:LANES, 512:WIDTH] = own.astype(BF)
     rhs_ref[LANES:256, 512:WIDTH] = jnp.zeros((LANES, SEG), BF)

time: 59.1 us -> 59 us (level)
  no operation moved by 1% of the time
where the time goes in v6:
time: 59 us; the launch traced here: 58.5 us
  starting transfers between devices  32.5 us (55%)
  waiting for transfers between devices  9.86 us (17%)
  blocking collectives  9.06 us (15%)
  Pallas kernels  5.75 us (10%)
  between operations  0.72 us (1%)
  other arithmetic  0.65 us (1%)
    all_to_all x1, starting transfers between devices, body(): ghosts = lax.all_to_all(pick(got), ('y', 'z'), 0, 0, tiled=True)  12.2 us
    all_to_all x1, waiting for transfers between devices, body(): ghosts = lax.all_to_all(pick(got), ('y', 'z'), 0, 0, tiled=True)  9.85 us
    all_to_all x1, starting transfers between devices, body(): got = lax.all_to_all(message, ('c', 'x'), 0, 0, tiled=True)  9.18 us
    all_to_all x1, blocking collectives, body(): parts = lax.all_to_all(sums, 'x', 0, 0, tiled=True)  9.06 us
    ppermute x1, starting transfers between devices, body(): lax.ppermute(across, 'x', [(i, (i + 2) % SUBS) for i in range(SUBS)])  4.72 us
    pallas_call x1, Pallas kernels, upward(): pl.pallas_call(upward_kernel, out_shape=(jax.ShapeDtypeStruct((ROWS, NODE...  2.75 us
    ppermute x1, starting transfers between devices, body(): second = lax.ppermute(second, 'c', [(0, 1), (1, 0)])  2.41 us
    ppermute x1, starting transfers between devices, body(): side = lax.ppermute(side, ('c', 'x'), steps)  2.01 us
  transfers between devices with their start and end apart: 6, of which 1 were waited for; matrix products, arithmetic and copies ran while one was open for 0% of the time, Pallas kernels for 2%

profile of v6, /device:TPU:2, one launch (start us, length us, event | category | flops | bytes accessed | tf_op | source)
XLA Modules:
  0.0 58.5 jit_solution(10648682395291144823)
XLA Ops:
  0.6 2.7 %upward.1 = (bf16[32,512]{1,0:T(8,128)(2,1)}, bf16[8,48,128]{2,1,0:T(8,128)(2,1)}, bf16[4,512,128]{2,1,0:T(8,128)(2,1)S(1)}, bf16[4,512,128]{2,1,0:T(8,128)(2,1)S(1)}, bf16[2,512,128]{2,1,0:T(8,128)(2,1)S(1)}) custom-call(s32[1,4]{1,0:T(1,128)} %count_hbm.1, bf16[256,512]{1,0:T(8,128)(2,1)} %leaves_hbm.1, s32[1,4,128]{2,1,0:T(4,128)} %target_hbm.1, ...), custom_call_target="tpu_custom_call" | custom-call | flops 134217728 | bytes 5242880 | tf_op jit(solution)/shard_map/upward/pallas_call | solution.py:136
  3.4 9.2 %all-to-all-start = ((bf16[8,48,128]{2,1,0:T(8,128)(2,1)}), bf16[8,48,128]{2,1,0:T(8,128)(2,1)S(1)}, u32[]{:S(2)}, u32[]{:S(2)}) async-start(bf16[8,48,128]{2,1,0:T(8,128)(2,1)} %get-tuple-element.11), calls=%async_computation | async-start | bytes 196608 | tf_op jit(solution)/shard_map/all_to_all | solution.py:272
  12.6 2.0 %collective-permute-start = (bf16[4,512,128]{2,1,0:T(8,128)(2,1)S(1)}, bf16[4,512,128]{2,1,0:T(8,128)(2,1)S(1)}, u32[]{:S(2)}, u32[]{:S(2)}) collective-permute-start(bf16[4,512,128]{2,1,0:T(8,128)(2,1)S(1)} %get-tuple-element.12), channel_id=1, source_target_pairs={{0,3},{1,0},{2,1},{3,2},{4,5},{5,6},{6,7},{7,4},{8,11},{9,8},{10,9... | collective-permute-start | bytes 1572872 | tf_op jit(solution)/shard_map/ppermute | solution.py:274
  14.6 4.7 %collective-permute-start.1 = (bf16[2,512,128]{2,1,0:T(8,128)(2,1)S(1)}, bf16[2,512,128]{2,1,0:T(8,128)(2,1)S(1)}, u32[]{:S(2)}, u32[]{:S(2)}) collective-permute-start(bf16[2,512,128]{2,1,0:T(8,128)(2,1)S(1)} %get-tuple-element.13), channel_id=1, source_target_pairs={{0,2},{1,3},{2,0},{3,1},{4,6},{5,7},{6,4},{7,5},{8,10},{9,11},{10,... | collective-permute-start | bytes 786440 | tf_op jit(solution)/shard_map/ppermute | solution.py:275
  19.3 0.0 all-to-all-done.got_ref
  19.3 1.2 %pick.1 = bf16[1024,128]{1,0:T(8,128)(2,1)} custom-call(bf16[8,48,128]{2,1,0:T(8,128)(2,1)S(1)} %all-to-all-done.got_ref), custom_call_target="tpu_custom_call" | custom-call | flops 17179869184 | bytes 524288 | tf_op jit(solution)/shard_map/pick/pallas_call | solution.py:178
  20.5 12.2 %all-to-all-start.1 = ((bf16[64,16,128]{2,1,0:T(8,128)(2,1)}), bf16[64,16,128]{2,1,0:T(8,128)(2,1)S(1)}, u32[]{:S(2)}, u32[]{:S(2)}) async-start(bf16[64,16,128]{2,1,0:T(8,128)(2,1)} %bitcast.2), calls=%async_computation.1 | async-start | bytes 524288 | tf_op jit(solution)/shard_map/all_to_all | solution.py:276
  32.8 0.0 collective-permute-done.1.across_ref
  32.8 0.0 collective-permute-done.side_ref
  32.8 0.1 plan.1
  32.9 1.9 %collective-permute-start.2 = (bf16[3,512,128]{2,1,0:T(8,128)(2,1)S(1)}, bf16[3,512,128]{2,1,0:T(8,128)(2,1)S(1)}, u32[]{:S(2)}, u32[]{:S(2)}) collective-permute-start(bf16[3,512,128]{2,1,0:T(8,128)(2,1)S(1)} %get-tuple-element.16), channel_id=1, source_target_pairs={{0,4},{4,0},{1,5},{5,1},{2,6},{6,2},{3,7},{7,3},{8,12},{12,8},{9,1... | collective-permute-start | bytes 1179656 | tf_op jit(solution)/shard_map/ppermute | solution.py:278
  34.8 2.4 %collective-permute-start.3 = (bf16[3,512,128]{2,1,0:T(8,128)(2,1)S(1)}, bf16[3,512,128]{2,1,0:T(8,128)(2,1)S(1)}, u32[]{:S(2)}, u32[]{:S(2)}) collective-permute-start(bf16[3,512,128]{2,1,0:T(8,128)(2,1)S(1)} %get-tuple-element.17), channel_id=1, source_target_pairs={{0,4},{4,0},{1,5},{5,1},{2,6},{6,2},{3,7},{7,3},{8,12},{12,8},{9,1... | collective-permute-start | bytes 1179656 | tf_op jit(solution)/shard_map/ppermute | solution.py:279
  37.2 9.8 %all-to-all-done.1 = bf16[64,16,128]{2,1,0:T(8,128)(2,1)S(1)} async-done(((bf16[64,16,128]{2,1,0:T(8,128)(2,1)}), bf16[64,16,128]{2,1,0:T(8,128)(2,1)S(1)}, u32[]{:S(2)}, u32[]{:S(2)}) %all-to-all-start.1) | async-done | bytes 262176 | tf_op jit(solution)/shard_map/all_to_all | solution.py:276
  47.1 0.0 collective-permute-done.2.first_ref
  47.1 0.0 collective-permute-done.3.second_ref
  47.1 1.7 %local_sums.1 = bf16[128,512]{1,0:T(8,128)(2,1)S(1)} custom-call(bf16[8,48,128]{2,1,0:T(8,128)(2,1)S(1)} %all-to-all-done.got_ref, bf16[1024,128]{1,0:T(8,128)(2,1)S(1)} %bitcast.6, s32[32,128]{1,0:T(8,128)S(1)} %get-tuple-element.14.plan_ref, bf16[4,512,128]{2,1,0:T(8,128)(2,1)S(1)} %get-tuple-element.15.own_ref, ...), custom_call_target="tpu_custom_call" | custom-call | flops 1073741824 | bytes 5242880 | tf_op jit(solution)/shard_map/local_sums/pallas_call | solution.py:253
  48.8 9.1 %all_to_all.25 = bf16[4,32,512]{2,1,0:T(8,128)(2,1)S(1)} all-to-all(bf16[4,32,512]{2,1,0:T(8,128)(2,1)S(1)} %bitcast.7), channel_id=1, replica_groups=mesh['y'=8,'z'=8,'c'=2,'x'=4] {'x'}, dimensions={0} | all-to-all | bytes 262144 | tf_op jit(solution)/shard_map/all_to_all | solution.py:281
  57.9 0.6 %convert_reduce_fusion = f32[32,512]{1,0:T(8,128)} fusion(bf16[4,32,512]{2,1,0:T(8,128)(2,1)S(1)} %all_to_all.25), kind=kLoop, calls=%fused_computation | loop fusion | flops 114688 | bytes 196608 | tf_op jit(solution)/shard_map/reduce_sum | solution.py:282
Async XLA Ops:
  3.4 15.9 %all-to-all-start = ((bf16[8,48,128]{2,1,0:T(8,128)(2,1)}), bf16[8,48,128]{2,1,0:T(8,128)(2,1)S(1)}, u32[]{:S(2)}, u32[]{:S(2)}) async-start(bf16[8,48,128]{2,1,0:T(8,128)(2,1)} %get-tuple-element.11), calls=%async_computation | async-start | bytes 196608 | tf_op jit(solution)/shard_map/all_to_all | solution.py:272
  12.6 20.2 %collective-permute-start = (bf16[4,512,128]{2,1,0:T(8,128)(2,1)S(1)}, bf16[4,512,128]{2,1,0:T(8,128)(2,1)S(1)}, u32[]{:S(2)}, u32[]{:S(2)}) collective-permute-start(bf16[4,512,128]{2,1,0:T(8,128)(2,1)S(1)} %get-tuple-element.12), channel_id=1, source_target_pairs={{0,3},{1,0},{2,1},{3,2},{4,5},{5,6},{6,7},{7,4},{8,11},{9,8},{10,9... | collective-permute-start | bytes 1572872 | tf_op jit(solution)/shard_map/ppermute | solution.py:274
  14.6 18.2 %collective-permute-start.1 = (bf16[2,512,128]{2,1,0:T(8,128)(2,1)S(1)}, bf16[2,512,128]{2,1,0:T(8,128)(2,1)S(1)}, u32[]{:S(2)}, u32[]{:S(2)}) collective-permute-start(bf16[2,512,128]{2,1,0:T(8,128)(2,1)S(1)} %get-tuple-element.13), channel_id=1, source_target_pairs={{0,2},{1,3},{2,0},{3,1},{4,6},{5,7},{6,4},{7,5},{8,10},{9,11},{10,... | collective-permute-start | bytes 786440 | tf_op jit(solution)/shard_map/ppermute | solution.py:275
  20.5 26.5 %all-to-all-start.1 = ((bf16[64,16,128]{2,1,0:T(8,128)(2,1)}), bf16[64,16,128]{2,1,0:T(8,128)(2,1)S(1)}, u32[]{:S(2)}, u32[]{:S(2)}) async-start(bf16[64,16,128]{2,1,0:T(8,128)(2,1)} %bitcast.2), calls=%async_computation.1 | async-start | bytes 524288 | tf_op jit(solution)/shard_map/all_to_all | solution.py:276
  32.9 14.2 %collective-permute-start.2 = (bf16[3,512,128]{2,1,0:T(8,128)(2,1)S(1)}, bf16[3,512,128]{2,1,0:T(8,128)(2,1)S(1)}, u32[]{:S(2)}, u32[]{:S(2)}) collective-permute-start(bf16[3,512,128]{2,1,0:T(8,128)(2,1)S(1)} %get-tuple-element.16), channel_id=1, source_target_pairs={{0,4},{4,0},{1,5},{5,1},{2,6},{6,2},{3,7},{7,3},{8,12},{12,8},{9,1... | collective-permute-start | bytes 1179656 | tf_op jit(solution)/shard_map/ppermute | solution.py:278
  34.8 12.3 %collective-permute-start.3 = (bf16[3,512,128]{2,1,0:T(8,128)(2,1)S(1)}, bf16[3,512,128]{2,1,0:T(8,128)(2,1)S(1)}, u32[]{:S(2)}, u32[]{:S(2)}) collective-permute-start(bf16[3,512,128]{2,1,0:T(8,128)(2,1)S(1)} %get-tuple-element.17), channel_id=1, source_target_pairs={{0,4},{4,0},{1,5},{5,1},{2,6},{6,2},{3,7},{7,3},{8,12},{12,8},{9,1... | collective-permute-start | bytes 1179656 | tf_op jit(solution)/shard_map/ppermute | solution.py:279
